TPU v7x, 128 devices: a whole 4x4x4 slice. The times are simulated.
128 devices in a mesh: gx: 16 (over y, x), gy: 8 (over z, core).
Axes of the slice: x: 4, y: 4, z: 4, core: 2. Of those that a mesh axis runs over, the one named last changes fastest.
Arguments:
- nodes: bfloat16 [262144, 256], P(('gx', 'gy')), may hold values from -6 to 6
- boundary_rows: int32 [16384], P(('gx', 'gy')), may hold values from 0 to 2047
- edge_source: int32 [4096, 128], P(('gx', 'gy')), may hold values from 0 to 2559
- edge_target: int32 [4096, 128], P(('gx', 'gy')), may hold values from 0 to 2047
- edge_mask: int32 [4096, 128], P(('gx', 'gy')), may hold values 0 or 1
- segment_ids: int32 [262144], P(('gx', 'gy')), may hold values from 0 to 511
- w_first: bfloat16 [512, 512], replicated, may hold values from -0.25 to 0.25
- b_first: float32 [512], replicated, may hold values from -3 to 3
- w_second: bfloat16 [512, 256], replicated, may hold values from -0.25 to 0.25
- cotangent: bfloat16 [4096, 256], P(('gx', 'gy')), may hold values from -6 to 6
Outputs:
- pooled: bfloat16 [4096, 256], P(('gx', 'gy'))
- grad_nodes: bfloat16 [262144, 256], P(('gx', 'gy'))
- grad_first: float32 [512, 512], replicated
- grad_bias: float32 [512], replicated
- grad_second: float32 [512, 256], replicated
All inputs are finite; a program needn't handle non-finite values. No bound on the sum of `edge_mask` on one device may be relied on, other than what follows from the above.
Results may differ from a plain program's by a relative error of at most 0.0043.
Values may be sent and summed in bfloat16 or wider, within the bound.
A program may use at most 128 MiB of HBM per device.

v0:
```python
import math

import jax
import jax.numpy as jnp
from jax import lax
from jax.sharding import PartitionSpec as P


def with_halo(block, sides, width):
    for axis, dim in sides:
        count = lax.axis_size(axis)
        forward = [(i, i + 1) for i in range(count - 1)]
        backward = [(target, source) for source, target in forward]
        low = lax.ppermute(
            lax.slice_in_dim(block, block.shape[dim] - width, None, axis=dim), axis, forward
        )
        high = lax.ppermute(lax.slice_in_dim(block, 0, width, axis=dim), axis, backward)
        block = jnp.concatenate([low, block, high], axis=dim)
    return block


def from_behind(array, axis, by):
    peers = lax.axis_size(axis)
    pairs = [(i, i + by) for i in range(peers) if 0 <= i + by < peers]
    return lax.ppermute(array, axis, pairs)


def local(
    nodes,
    boundary_rows,
    edge_source,
    edge_target,
    edge_mask,
    segment_ids,
    w_first,
    b_first,
    w_second,
    cotangent,
):
    count_x = lax.axis_size("gx")
    count_y = lax.axis_size("gy")
    node_count = nodes.shape[0]
    features = nodes.shape[1]
    bnd_count = boundary_rows.shape[0]
    seg_rows = cotangent.shape[0]
    table_rows = node_count + 4 * bnd_count
    boundary = nodes[boundary_rows]
    framed = with_halo(boundary[None, None], (("gx", 0), ("gy", 1)), 1)
    row_table = jnp.concatenate([nodes, framed[0, 1], framed[2, 1], framed[1, 0], framed[1, 2]], 0)
    source_ids = edge_source.reshape(-1)
    target_ids = edge_target.reshape(-1)
    edge_total = source_ids.shape[0]
    per_group = 128 * math.gcd(edge_total // 128, 4)
    group_count = edge_total // per_group
    table_iota = jnp.arange(table_rows, dtype=jnp.int32)
    live_mask = edge_mask.reshape(-1).astype(jnp.float32)[:, None]
    inputs = jnp.concatenate([row_table[source_ids], row_table[target_ids]], 1)
    preact = jnp.dot(inputs, w_first, preferred_element_type=jnp.float32) + b_first
    hidden = jax.nn.gelu(preact).astype(jnp.bfloat16)
    message = (jnp.dot(hidden, w_second, preferred_element_type=jnp.float32) * live_mask).astype(
        jnp.bfloat16
    )
    contract_rows = (((0,), (0,)), ((), ()))

    def incoming_step(total, packed):
        targets_block, messages_block = packed
        chosen = (targets_block[:, None] == table_iota[None, :node_count]).astype(jnp.bfloat16)
        return (
            total
            + lax.dot_general(
                chosen, messages_block, contract_rows, preferred_element_type=jnp.float32
            ),
            None,
        )

    incoming, unused_one = lax.scan(
        incoming_step,
        jnp.zeros((node_count, features), jnp.float32),
        (
            target_ids.reshape(group_count, per_group),
            message.reshape(group_count, per_group, features),
        ),
    )
    updated = (nodes.astype(jnp.float32) + incoming).astype(jnp.bfloat16)
    segment_iota = jnp.arange(count_x * seg_rows, dtype=jnp.int32)
    segment_table = (segment_ids[:, None] == segment_iota[None, :]).astype(jnp.bfloat16)
    partial_sums = lax.dot_general(
        segment_table, updated, contract_rows, preferred_element_type=jnp.float32
    )
    pooled = lax.psum_scatter(partial_sums, "gx", scatter_dimension=0, tiled=True).astype(
        jnp.bfloat16
    )
    line_rows = lax.all_gather(cotangent, "gx", axis=0, tiled=True)
    grad_updated = jnp.dot(segment_table, line_rows, preferred_element_type=jnp.float32)
    grad_message = (grad_updated[target_ids] * live_mask).astype(jnp.bfloat16)
    grad_second = lax.dot_general(
        hidden, grad_message, contract_rows, preferred_element_type=jnp.float32
    )
    grad_hidden = lax.dot_general(
        grad_message, w_second, (((1,), (1,)), ((), ())), preferred_element_type=jnp.float32
    )
    unused, pull_back = jax.vjp(jax.nn.gelu, preact)
    grad_pre = pull_back(grad_hidden)[0].astype(jnp.bfloat16)
    grad_bias = jnp.sum(grad_pre.astype(jnp.float32), 0)
    grad_first = lax.dot_general(
        inputs, grad_pre, contract_rows, preferred_element_type=jnp.float32
    )
    grad_inputs = lax.dot_general(
        grad_pre, w_first, (((1,), (1,)), ((), ())), preferred_element_type=jnp.float32
    ).astype(jnp.bfloat16)

    def table_step(total, packed):
        sources_block, targets_block, grads_block = packed
        from_source = (sources_block[:, None] == table_iota[None, :]).astype(jnp.bfloat16)
        from_target = (targets_block[:, None] == table_iota[None, :]).astype(jnp.bfloat16)
        total = total + lax.dot_general(
            from_source,
            grads_block[:, :features],
            contract_rows,
            preferred_element_type=jnp.float32,
        )
        total = total + lax.dot_general(
            from_target,
            grads_block[:, features:],
            contract_rows,
            preferred_element_type=jnp.float32,
        )
        return (total, None)

    grad_table, unused_two = lax.scan(
        table_step,
        jnp.zeros((table_rows, features), jnp.float32),
        (
            source_ids.reshape(group_count, per_group),
            target_ids.reshape(group_count, per_group),
            grad_inputs.reshape(group_count, per_group, 2 * features),
        ),
    )
    slots = grad_table[node_count:].reshape(4, bnd_count, features)
    returned = jnp.zeros((bnd_count, features), jnp.float32)
    for direction, slot_index in ((-1, 0), (1, 1)):
        returned = returned + from_behind(
            slots[slot_index].astype(jnp.bfloat16), "gx", direction
        ).astype(jnp.float32)
    for direction, slot_index in ((-1, 2), (1, 3)):
        returned = returned + from_behind(
            slots[slot_index].astype(jnp.bfloat16), "gy", direction
        ).astype(jnp.float32)
    boundary_table = (boundary_rows[:, None] == table_iota[None, :node_count]).astype(jnp.float32)
    spread_back = lax.dot_general(
        boundary_table,
        returned,
        contract_rows,
        precision=lax.Precision.HIGHEST,
        preferred_element_type=jnp.float32,
    )
    grad_nodes = grad_updated + grad_table[:node_count] + spread_back
    grad_first, grad_bias, grad_second = lax.psum(
        (grad_first, grad_bias, grad_second), ("gx", "gy")
    )
    edge_scale = 1.0 / jnp.sqrt(jnp.float32(edge_total * count_x * count_y))
    return (
        pooled,
        grad_nodes.astype(jnp.bfloat16),
        grad_first * edge_scale,
        grad_bias * edge_scale,
        grad_second * edge_scale,
    )


def solution(mesh):
    in_specs = (
        P(("gx", "gy"), None),
        P(("gx", "gy")),
        P(("gx", "gy"), None),
        P(("gx", "gy"), None),
        P(("gx", "gy"), None),
        P(("gx", "gy")),
        P(),
        P(),
        P(),
        P(("gx", "gy"), None),
    )
    out_specs = (P(("gx", "gy"), None), P(("gx", "gy"), None), P(), P(), P())
    return jax.shard_map(local, mesh=mesh, in_specs=in_specs, out_specs=out_specs, check_vma=False)
```

profile of v0, /device:TPU:1, one launch (start us, length us, event | category | flops | bytes accessed | tf_op | source)
XLA Modules:
  0.0 394.8 jit_solution(15080129725975297688)
XLA Ops:
  10.9 3.9 collective-permute-start
  20.4 21.5 %all_gather.3 = bf16[512,256]{1,0:T(8,128)(2,1)S(1)} all-gather(bf16[32,256]{1,0:T(8,128)(2,1)} %param.23), channel_id=1, replica_groups=mesh['gx'=16,'gy'=8] {'gx'}, dimensions={0}, use_global_device_ids=true | all-gather | bytes 278528 | tf_op jit(solution)/shard_map/all_gather | solution.py:93
  45.3 17.7 %gather_fusion.3 = f32[4096,256]{1,0:T(8,128)} fusion(f32[2048,256]{1,0:T(8,128)} %fusion.28, s32[4096]{0:T(1024)S(1)} %broadcast_clamp_fusion), kind=kCustom, calls=%fused_computation.3 | custom fusion | bytes 8404992 | tf_op jit(solution)/shard_map/gather | solution.py:95
  63.1 9.9 %collective-permute-start.2 = (bf16[3,1,128,256]{3,2,1,0:T(8,128)(2,1)S(1)}, bf16[3,1,128,256]{3,2,1,0:T(8,128)(2,1)S(1)}, u32[]{:S(2)}, u32[]{:S(2)}) collective-permute-start(bf16[3,1,128,256]{3,2,1,0:T(8,128)(2,1)S(1)} %pad_maximum_fusion), channel_id=1, source_target_pairs={{0,1},{1,2},{2,3},{3,4},{4,5},{5,6},{6,7},{8,9},{9,10},{10,11},{11... | collective-permute-start | bytes 589832 | tf_op jit(solution)/shard_map/ppermute | solution.py:14
  75.6 4.4 %collective-permute-done.3 = bf16[3,1,128,256]{3,2,1,0:T(8,128)(2,1)S(1)} collective-permute-done((bf16[3,1,128,256]{3,2,1,0:T(8,128)(2,1)S(1)}, bf16[3,1,128,256]{3,2,1,0:T(8,128)(2,1)S(1)}, u32[]{:S(2)}, u32[]{:S(2)}) %collective-permute-start.3) | collective-permute-done | bytes 196640 | tf_op jit(solution)/shard_map/ppermute | solution.py:17
  80.0 17.1 %gather_fusion.1 = bf16[4096,256]{1,0:T(8,128)(2,1)} fusion(bf16[2560,256]{1,0:T(8,128)(2,1)S(1)} %fusion.43, s32[4096]{0:T(1024)S(1)} %get-tuple-element.158), kind=kCustom, calls=%fused_computation.1 | custom fusion | bytes 4210688 | tf_op jit(solution)/shard_map/gather | solution.py:57
  97.0 3.1 constant_dynamic-update-slice_fusion.2
  100.2 17.1 %gather_fusion.2 = bf16[4096,256]{1,0:T(8,128)(2,1)} fusion(bf16[2560,256]{1,0:T(8,128)(2,1)S(1)} %fusion.43, s32[4096]{0:T(1024)S(1)} %get-tuple-element.157), kind=kCustom, calls=%fused_computation.2 | custom fusion | bytes 4210688 | tf_op jit(solution)/shard_map/gather | solution.py:57
  117.2 3.1 constant_dynamic-update-slice_fusion.1
  120.3 6.2 %multiply_convert_fusion = (bf16[4096,512]{1,0:T(8,128)(2,1)S(1)}, f32[4096,512]{1,0:T(8,128)S(1)}) fusion(f32[512]{0:T(512)S(1)} %copy-done.11, bf16[4096,512]{1,0:T(8,128)(2,1)} %constant_dynamic-update-slice_fusion.1, bf16[512,512]{1,0:T(8,128)(2,1)S(1)} %copy-done), kind=kOutput, calls=%fused_computation.37 | convolution fusion | flops 2168455168 | bytes 17303552 | tf_op jit(solution)/shard_map/dot_general | solution.py:58
  126.6 8.4 %convert_reduce_fusion = (f32[512]{0:T(512)S(1)}, bf16[4096,512]{1,0:T(8,128)(2,1)S(1)}) fusion(f32[4096,512]{1,0:T(8,128)S(1)} %get-tuple-element.154, f32[512]{0:T(512)S(1)} %copy-done.11, bf16[512,256]{1,0:T(8,128)(2,1)S(1)} %copy-done.9, f32[4096,256]{1,0:T(8,128)S(1)} %copy-done.6, f32[4096]{0:T(1024)S(1)} %convert_bitcast_fusion), kind=kOutput, calls=%fused_computation.36 | convolution fusion | flops 1124072960 | bytes 17059840 | tf_op jit(solution)/shard_map/dot_general | solution.py:99
  135.0 3.3 fusion.47
  138.3 4.3 %convolution_convert_fusion = bf16[4096,512]{1,0:T(8,128)(2,1)} fusion(bf16[4096,512]{1,0:T(8,128)(2,1)S(1)} %get-tuple-element.156, bf16[512,512]{1,0:T(8,128)(2,1)S(1)} %copy-done), kind=kOutput, calls=%fused_computation.38 | convolution fusion | flops 2149580800 | bytes 8912896 | tf_op jit(solution)/shard_map/dot_general | solution.py:108
  142.6 2.8 fusion.45
  145.4 5.0 %fusion.27 = bf16[4096,256]{1,0:T(8,128)(2,1)} fusion(bf16[4096,512]{1,0:T(8,128)(2,1)} %copy-done.7, bf16[512,256]{1,0:T(8,128)(2,1)S(1)} %copy-done.9, f32[4096]{0:T(1024)S(1)} %convert_bitcast_fusion), kind=kOutput, calls=%fused_computation.40 | convolution fusion | flops 1075838976 | bytes 6569984 | tf_op jit(solution)/shard_map/dot_general | solution.py:60
  150.4 50.7 %while.24 = (s32[]{:T(128)}, f32[2560,256]{1,0:T(8,128)S(1)}, s32[8,512]{1,0:T(8,128)S(1)}, bf16[8,512,512]{2,1,0:T(8,128)(2,1)}, s32[8,512]{1,0:T(8,128)S(1)}, /*index=5*/s32[]{:T(128)}, s32[]{:T(128)}) while((s32[]{:T(128)}, f32[2560,256]{1,0:T(8,128)S(1)}, s32[8,512]{1,0:T(8,128)S(1)}, ...), condition=%wide.region_4.5_spmd.clone.clone, body=%wide.region_3.4_spmd.clone.clone.sunk | while | flops 1346764800 | bytes 14168187 | solution.py:130
  203.4 4.0 %collective-permute-start.5 = (bf16[128,256]{1,0:T(8,128)(2,1)}, bf16[128,256]{1,0:T(8,128)(2,1)S(1)}, u32[]{:S(2)}, u32[]{:S(2)}) collective-permute-start(bf16[128,256]{1,0:T(8,128)(2,1)} %get-tuple-element.150), channel_id=1, source_target_pairs={{0,8},{8,16},{16,24},{24,32},{32,40},{40,48},{48,56},{56,64},{64,7... | collective-permute-start | bytes 196616 | tf_op jit(solution)/shard_map/ppermute | solution.py:25
  209.3 3.6 collective-permute-start.7
  213.1 34.9 %while.23 = (s32[]{:T(128)}, f32[2048,256]{1,0:T(8,128)}, s32[8,512]{1,0:T(8,128)S(1)}, s32[2560]{0:T(1024)S(1)}, bf16[8,512,256]{2,1,0:T(8,128)(2,1)}, /*index=5*/s32[]{:T(128)}, s32[]{:T(128)}) while((s32[]{:T(128)}, f32[2048,256]{1,0:T(8,128)}, s32[8,512]{1,0:T(8,128)S(1)}, s32[2560]{0:T(1024)S(1)}, ...), condition=%wide.region_1.2_spmd.clone, body=%wide.region_0.1_spmd.clone.sunk | while | flops 538968064 | bytes 4487771 | solution.py:76
  213.1 3.7 fusion.68
  216.8 4.4 %fusion.68 = f32[2048,256]{1,0:T(8,128)} fusion(f32[2048,256]{1,0:T(8,128)} %get-tuple-element.233, s32[2048]{0:T(1024)S(1)} %slice.93, s32[512]{0:T(512)S(1)} %bitcast.58, pred[]{:T(512)S(6)} %compare.6, bf16[8,512,256]{2,1,0:T(8,128)(2,1)} %get-tuple-element.243, s32[]{:T(128)} %get-tuple-element.232), kind=kOutput, calls=%fused_computation.7.clone.1 | convolution fusion | flops 538968064 | bytes 4467201 | tf_op jit(solution)/shard_map/while/body/eval_jaxpr/dot_general | solution.py:70
  221.2 4.5 %fusion.68 = f32[2048,256]{1,0:T(8,128)} fusion(f32[2048,256]{1,0:T(8,128)} %get-tuple-element.233, s32[2048]{0:T(1024)S(1)} %slice.93, s32[512]{0:T(512)S(1)} %bitcast.58, pred[]{:T(512)S(6)} %compare.6, bf16[8,512,256]{2,1,0:T(8,128)(2,1)} %get-tuple-element.243, s32[]{:T(128)} %get-tuple-element.232), kind=kOutput, calls=%fused_computation.7.clone.1 | convolution fusion | flops 538968064 | bytes 4467201 | tf_op jit(solution)/shard_map/while/body/eval_jaxpr/dot_general | solution.py:70
  225.8 4.4 %fusion.68 = f32[2048,256]{1,0:T(8,128)} fusion(f32[2048,256]{1,0:T(8,128)} %get-tuple-element.233, s32[2048]{0:T(1024)S(1)} %slice.93, s32[512]{0:T(512)S(1)} %bitcast.58, pred[]{:T(512)S(6)} %compare.6, bf16[8,512,256]{2,1,0:T(8,128)(2,1)} %get-tuple-element.243, s32[]{:T(128)} %get-tuple-element.232), kind=kOutput, calls=%fused_computation.7.clone.1 | convolution fusion | flops 538968064 | bytes 4467201 | tf_op jit(solution)/shard_map/while/body/eval_jaxpr/dot_general | solution.py:70
  230.2 4.4 %fusion.68 = f32[2048,256]{1,0:T(8,128)} fusion(f32[2048,256]{1,0:T(8,128)} %get-tuple-element.233, s32[2048]{0:T(1024)S(1)} %slice.93, s32[512]{0:T(512)S(1)} %bitcast.58, pred[]{:T(512)S(6)} %compare.6, bf16[8,512,256]{2,1,0:T(8,128)(2,1)} %get-tuple-element.243, s32[]{:T(128)} %get-tuple-element.232), kind=kOutput, calls=%fused_computation.7.clone.1 | convolution fusion | flops 538968064 | bytes 4467201 | tf_op jit(solution)/shard_map/while/body/eval_jaxpr/dot_general | solution.py:70
  234.7 4.4 %fusion.68 = f32[2048,256]{1,0:T(8,128)} fusion(f32[2048,256]{1,0:T(8,128)} %get-tuple-element.233, s32[2048]{0:T(1024)S(1)} %slice.93, s32[512]{0:T(512)S(1)} %bitcast.58, pred[]{:T(512)S(6)} %compare.6, bf16[8,512,256]{2,1,0:T(8,128)(2,1)} %get-tuple-element.243, s32[]{:T(128)} %get-tuple-element.232), kind=kOutput, calls=%fused_computation.7.clone.1 | convolution fusion | flops 538968064 | bytes 4467201 | tf_op jit(solution)/shard_map/while/body/eval_jaxpr/dot_general | solution.py:70
  239.1 4.4 %fusion.68 = f32[2048,256]{1,0:T(8,128)} fusion(f32[2048,256]{1,0:T(8,128)} %get-tuple-element.233, s32[2048]{0:T(1024)S(1)} %slice.93, s32[512]{0:T(512)S(1)} %bitcast.58, pred[]{:T(512)S(6)} %compare.6, bf16[8,512,256]{2,1,0:T(8,128)(2,1)} %get-tuple-element.243, s32[]{:T(128)} %get-tuple-element.232), kind=kOutput, calls=%fused_computation.7.clone.1 | convolution fusion | flops 538968064 | bytes 4467201 | tf_op jit(solution)/shard_map/while/body/eval_jaxpr/dot_general | solution.py:70
  243.6 4.4 %fusion.68 = f32[2048,256]{1,0:T(8,128)} fusion(f32[2048,256]{1,0:T(8,128)} %get-tuple-element.233, s32[2048]{0:T(1024)S(1)} %slice.93, s32[512]{0:T(512)S(1)} %bitcast.58, pred[]{:T(512)S(6)} %compare.6, bf16[8,512,256]{2,1,0:T(8,128)(2,1)} %get-tuple-element.243, s32[]{:T(128)} %get-tuple-element.232), kind=kOutput, calls=%fused_computation.7.clone.1 | convolution fusion | flops 538968064 | bytes 4467201 | tf_op jit(solution)/shard_map/while/body/eval_jaxpr/dot_general | solution.py:70
  248.0 65.8 %psum.22 = f32[512]{0:T(512)S(1)} all-reduce(f32[512]{0:T(512)S(1)} %get-tuple-element.155), channel_id=1, replica_groups=mesh['gx'=16,'gy'=8] {'gx','gy'}, use_global_device_ids=true, to_apply=%region_7.8 | all-reduce | flops 512 | bytes 4096 | tf_op jit(solution)/shard_map/psum | solution.py:158
  313.8 4.3 %fusion.29 = f32[512,256]{1,0:T(8,128)} fusion(s32[2048]{0:T(1024)S(1)} %copy-done.10, f32[2048,256]{1,0:T(8,128)} %get-tuple-element.67, bf16[2048,256]{1,0:T(8,128)(2,1)} %param.14), kind=kOutput, calls=%fused_computation.44 | convolution fusion | flops 539492352 | bytes 3678208 | tf_op jit(solution)/shard_map/dot_general | solution.py:87
  318.7 3.7 fusion.30
  322.4 40.7 %all-reduce.3.cloned.1.call-done = (f32[512,512]{1,0:T(8,128)}, f32[512,256]{1,0:T(8,128)}) async-done(((f32[512,512]{1,0:T(8,128)}, f32[512,256]{1,0:T(8,128)}), (f32[512,512]{1,0:T(8,128)}, f32[512,256]{1,0:T(8,128)})) %all-reduce.3.cloned.1.call-update) | async-done | bytes 1572880 | tf_op jit(solution)/shard_map/psum | solution.py:158
  367.2 18.8 %reduce-scatter.2.cloned.1.call-done = f32[32,256]{1,0:T(8,128)} async-done(((f32[512,256]{1,0:T(8,128)}), f32[32,256]{1,0:T(8,128)}) %reduce-scatter.2.cloned.1.call-update) | async-done | bytes 32784 | tf_op jit(solution)/shard_map/reduce_scatter | solution.py:90
  (128 shorter events, 75.3 us)
Async XLA Ops:
  8.0 112.3 %copy-start = (bf16[512,512]{1,0:T(8,128)(2,1)S(1)}, bf16[512,512]{1,0:T(8,128)(2,1)}, u32[]{:S(2)}) copy-start(bf16[512,512]{1,0:T(8,128)(2,1)} %param.20) | copy-start | bytes 1572868
  8.0 355.0 %all-reduce.3.cloned.1.call-start = ((), (), s32[]{:S(2)}) async-start(), calls=%async_computation.2 | async-start | bytes 3145728 | tf_op jit(solution)/shard_map/psum | solution.py:158
  10.9 52.2 %collective-permute-start = (bf16[1,1,128,256]{3,2,1,0:T(8,128)(2,1)S(1)}, bf16[1,1,128,256]{3,2,1,0:T(8,128)(2,1)S(1)}, u32[]{:S(2)}, u32[]{:S(2)}) collective-permute-start(bf16[1,1,128,256]{3,2,1,0:T(8,128)(2,1)S(1)} %bitcast.53), channel_id=1, source_target_pairs={{0,8},{8,16},{16,24},{24,32},{32,40},{40,48},{48,56},{56,64},{64,7... | collective-permute-start | bytes 196616 | tf_op jit(solution)/shard_map/ppermute | solution.py:14
  14.8 48.2 %collective-permute-start.1 = (bf16[1,1,128,256]{3,2,1,0:T(8,128)(2,1)S(1)}, bf16[1,1,128,256]{3,2,1,0:T(8,128)(2,1)S(1)}, u32[]{:S(2)}, u32[]{:S(2)}) collective-permute-start(bf16[1,1,128,256]{3,2,1,0:T(8,128)(2,1)S(1)} %bitcast.54), channel_id=1, source_target_pairs={{8,0},{16,8},{24,16},{32,24},{40,32},{48,40},{56,48},{64,56},{72,6... | collective-permute-start | bytes 196616 | tf_op jit(solution)/shard_map/ppermute | solution.py:17
  63.1 12.5 %collective-permute-start.2 = (bf16[3,1,128,256]{3,2,1,0:T(8,128)(2,1)S(1)}, bf16[3,1,128,256]{3,2,1,0:T(8,128)(2,1)S(1)}, u32[]{:S(2)}, u32[]{:S(2)}) collective-permute-start(bf16[3,1,128,256]{3,2,1,0:T(8,128)(2,1)S(1)} %pad_maximum_fusion), channel_id=1, source_target_pairs={{0,1},{1,2},{2,3},{3,4},{4,5},{5,6},{6,7},{8,9},{9,10},{10,11},{11... | collective-permute-start | bytes 589832 | tf_op jit(solution)/shard_map/ppermute | solution.py:14
  73.0 7.0 %collective-permute-start.3 = (bf16[3,1,128,256]{3,2,1,0:T(8,128)(2,1)S(1)}, bf16[3,1,128,256]{3,2,1,0:T(8,128)(2,1)S(1)}, u32[]{:S(2)}, u32[]{:S(2)}) collective-permute-start(bf16[3,1,128,256]{3,2,1,0:T(8,128)(2,1)S(1)} %pad_maximum_fusion), channel_id=1, source_target_pairs={{1,0},{2,1},{3,2},{4,3},{5,4},{6,5},{7,6},{9,8},{10,9},{11,10},{12... | collective-permute-start | bytes 589832 | tf_op jit(solution)/shard_map/ppermute | solution.py:17
  117.2 3.1 copy-start.11
  120.3 6.3 %copy-start.6 = (f32[4096,256]{1,0:T(8,128)S(1)}, f32[4096,256]{1,0:T(8,128)}, u32[]{:S(2)}) copy-start(f32[4096,256]{1,0:T(8,128)} %gather_fusion.3) | copy-start | bytes 12582916
  120.3 6.3 %copy-start.9 = (bf16[512,256]{1,0:T(8,128)(2,1)S(1)}, bf16[512,256]{1,0:T(8,128)(2,1)}, u32[]{:S(2)}) copy-start(bf16[512,256]{1,0:T(8,128)(2,1)} %param.22) | copy-start | bytes 786436
  126.5 16.1 %copy-start.7 = (bf16[4096,512]{1,0:T(8,128)(2,1)}, bf16[4096,512]{1,0:T(8,128)(2,1)S(1)}, u32[]{:S(2)}) copy-start(bf16[4096,512]{1,0:T(8,128)(2,1)S(1)} %get-tuple-element.153) | copy-start | bytes 12582916
  126.6 8.4 %copy-start.5 = (bf16[4096,512]{1,0:T(8,128)(2,1)S(1)}, bf16[4096,512]{1,0:T(8,128)(2,1)}, u32[]{:S(2)}) copy-start(bf16[4096,512]{1,0:T(8,128)(2,1)} %constant_dynamic-update-slice_fusion.1) | copy-start | bytes 12582916
  145.4 5.0 %copy-start.2 = (f32[2560,256]{1,0:T(8,128)S(1)}, f32[2560,256]{1,0:T(8,128)}, u32[]{:S(2)}) copy-start(f32[2560,256]{1,0:T(8,128)} %custom-call.1) | copy-start | bytes 7864324
  152.3 2.7 copy-start.4
  158.6 2.7 copy-start.4
  165.0 2.7 copy-start.4
  171.3 2.7 copy-start.4
  177.7 2.7 copy-start.4
  184.0 2.7 copy-start.4
  190.4 2.7 copy-start.4
  196.7 2.7 copy-start.4
  201.1 11.9 %copy-start.3 = (f32[2560,256]{1,0:T(8,128)}, f32[2560,256]{1,0:T(8,128)S(1)}, u32[]{:S(2)}) copy-start(f32[2560,256]{1,0:T(8,128)S(1)} %get-tuple-element.68) | copy-start | bytes 7864324
  202.1 116.5 %collective-permute-start.4 = (bf16[128,256]{1,0:T(8,128)(2,1)}, bf16[128,256]{1,0:T(8,128)(2,1)S(1)}, u32[]{:S(2)}, u32[]{:S(2)}) collective-permute-start(bf16[128,256]{1,0:T(8,128)(2,1)} %get-tuple-element.147), channel_id=1, source_target_pairs={{8,0},{16,8},{24,16},{32,24},{40,32},{48,40},{56,48},{64,56},{72,6... | collective-permute-start | bytes 196616 | tf_op jit(solution)/shard_map/ppermute | solution.py:25
  203.4 115.3 %collective-permute-start.5 = (bf16[128,256]{1,0:T(8,128)(2,1)}, bf16[128,256]{1,0:T(8,128)(2,1)S(1)}, u32[]{:S(2)}, u32[]{:S(2)}) collective-permute-start(bf16[128,256]{1,0:T(8,128)(2,1)} %get-tuple-element.150), channel_id=1, source_target_pairs={{0,8},{8,16},{16,24},{24,32},{32,40},{40,48},{48,56},{56,64},{64,7... | collective-permute-start | bytes 196616 | tf_op jit(solution)/shard_map/ppermute | solution.py:25
  207.4 111.3 %collective-permute-start.6 = (bf16[128,256]{1,0:T(8,128)(2,1)}, bf16[128,256]{1,0:T(8,128)(2,1)S(1)}, u32[]{:S(2)}, u32[]{:S(2)}) collective-permute-start(bf16[128,256]{1,0:T(8,128)(2,1)} %get-tuple-element.149), channel_id=1, source_target_pairs={{1,0},{2,1},{3,2},{4,3},{5,4},{6,5},{7,6},{9,8},{10,9},{11,10},{12... | collective-permute-start | bytes 196616 | tf_op jit(solution)/shard_map/ppermute | solution.py:25
  209.3 109.3 %collective-permute-start.7 = (bf16[128,256]{1,0:T(8,128)(2,1)S(1)}, bf16[128,256]{1,0:T(8,128)(2,1)S(1)}, u32[]{:S(2)}, u32[]{:S(2)}) collective-permute-start(bf16[128,256]{1,0:T(8,128)(2,1)S(1)} %get-tuple-element.148), channel_id=1, source_target_pairs={{0,1},{1,2},{2,3},{3,4},{4,5},{5,6},{6,7},{8,9},{9,10},{10,11},{11... | collective-permute-start | bytes 196616 | tf_op jit(solution)/shard_map/ppermute | solution.py:25
  213.0 173.0 %reduce-scatter.2.cloned.1.call-start = ((), (), s32[]{:S(2)}) async-start(), calls=%async_computation.1 | async-start | bytes 557056 | tf_op jit(solution)/shard_map/reduce_scatter | solution.py:90
  213.1 100.7 %copy-start.10 = (s32[2048]{0:T(1024)S(1)}, s32[2048]{0:T(1024)}, u32[]{:S(2)}) copy-start(s32[2048]{0:T(1024)} %param.19) | copy-start | bytes 24580
  248.0 70.7 %copy-start.1 = (f32[2048,256]{1,0:T(8,128)S(1)}, f32[2048,256]{1,0:T(8,128)}, u32[]{:S(2)}) copy-start(f32[2048,256]{1,0:T(8,128)} %fusion.28) | copy-start | bytes 6291460
  248.0 70.7 %copy-start.8 = (s32[128]{0:T(128)S(1)}, s32[128]{0:T(128)}, u32[]{:S(2)}) copy-start(s32[128]{0:T(128)} %param.15) | copy-start | bytes 1540
Sparse Core Ops, SparseCore 0:
  213.1 149.8 all-reduce.2
Sparse Core Ops, SparseCore 1:
  318.2 67.8 reduce-scatter.1
where the time goes:
time: 398 us; the launch traced here: 395 us
  matrix products  111 us (28%)
  blocking collectives  87.2 us (22%)
  local copies, waits for them, and re-layouts  79 us (20%)
  waiting for transfers between devices  64.4 us (16%)
  starting transfers between devices  28.1 us (7%)
  between operations  15.8 us (4%)
  other arithmetic  9.22 us (2%)
    psum x1, blocking collectives, local(): lax.psum((grad_first, grad_bias, grad_second), ('gx', 'gy'))  65.8 us
    psum x1, waiting for transfers between devices, local(): lax.psum((grad_first, grad_bias, grad_second), ('gx', 'gy'))  40.7 us
    dot_general x8, matrix products, incoming_step(): lax.dot_general(chosen, messages_block, contract_rows, preferred_element_...  34.8 us
    gather x2, local copies, waits for them, and re-layouts, local(): inputs = jnp.concatenate([row_table[source_ids], row_table[target_ids]], 1)  34.1 us
    dot_general x8, matrix products, table_step(): lax.dot_general(from_source, grads_block[:, :features], contract_rows, pr...  21.8 us
    all_gather x1, blocking collectives, local(): line_rows = lax.all_gather(cotangent, 'gx', axis=0, tiled=True)  21.5 us
    reduce_scatter x1, waiting for transfers between devices, local(): lax.psum_scatter(partial_sums, 'gx', scatter_dimension=0, tiled=True)  18.8 us
    gather x1, local copies, waits for them, and re-layouts, local(): grad_message = (grad_updated[target_ids] * live_mask).astype(jnp.bfloat16)  17.7 us
  transfers between devices with their start and end apart: 10, of which 4 were waited for; matrix products, arithmetic and copies ran while one was open for 18% of the time, Pallas kernels for 0%

commit v1 on v0

v1 whole, which is shorter than its diff:
```python
import functools

import jax
import jax.numpy as jnp
from jax import lax
from jax.experimental import pallas as pl
from jax.experimental.pallas import tpu as pltpu
from jax.sharding import PartitionSpec as P

MESH = pl.DeviceIdType.MESH
BF = jnp.bfloat16
F32 = jnp.float32
N = 2048
NB = 128
HALO = 4 * NB
F = 256
H = 512
E = 4096
SEG = 512
SR = 32
GX = 16
GY = 8
W = 1024
CH = 48
PW = 784
HW = H // 2
NT = (((1,), (1,)), ((), ()))


def dot(a, b):
    return jnp.dot(a, b, preferred_element_type=F32)


def dnt(a, b):
    return lax.dot_general(a, b, NT, preferred_element_type=F32)


def one_hot(row, first, count):
    rows = lax.broadcasted_iota(jnp.int32, (count, row.shape[1]), 0)
    return jnp.where(rows == row - first, 1.0, 0.0).astype(BF)


def id_row(ref, first, count):
    return jnp.concatenate([ref[pl.ds(first + i, 1), :] for i in range(count)], axis=1)


def eye(size):
    a = lax.broadcasted_iota(jnp.int32, (size, size), 0)
    b = lax.broadcasted_iota(jnp.int32, (size, size), 1)
    return jnp.where(a == b, 1.0, 0.0).astype(BF)


def split(value):
    high = value.astype(BF)
    return high, (value - high.astype(F32)).astype(BF)


def kernel(
    nodes,
    brows,
    src,
    tgt,
    mask,
    segs,
    w1,
    b1,
    w2,
    cot,
    pooled,
    gnodes,
    gw,
    tt,
    w1t,
    bcol,
    bnd,
    hrecv,
    line,
    line_t,
    xt,
    mseg,
    hid,
    gp,
    gi,
    pwf,
    pws,
    cbuf,
    csum,
    rsb,
    rsbias,
    zb,
    zbias,
    ag,
    psend,
    precv,
    gslot,
    gret,
    acc,
    h_s,
    h_r,
    c_s,
    c_r,
    p_s,
    p_r,
    g_s,
    g_r,
    core_s,
    core_r,
    rs_s,
    rs_r,
    rb_s,
    rb_r,
    z_s,
    z_r,
    zb_s,
    zb_r,
    ag_s,
    ag_r,
    agb_s,
    agb_r,
    fw_s,
    fw_r,
):
    me = lax.axis_index("gx")
    my = lax.axis_index("gy")
    core = lax.rem(my, 2)
    z = lax.div(my, 2)
    sib = my + 1 - 2 * core

    barrier = pltpu.get_barrier_semaphore()
    for d in range(1, GX):
        pl.semaphore_signal(
            barrier, inc=1, device_id={"gx": lax.rem(me + d, GX)}, device_id_type=MESH
        )
    for d in range(1, GY):
        pl.semaphore_signal(
            barrier, inc=1, device_id={"gy": lax.rem(my + d, GY)}, device_id_type=MESH
        )

    def remote(source, target, send, receive, device):
        return pltpu.make_async_remote_copy(
            src_ref=source,
            dst_ref=target,
            send_sem=send,
            recv_sem=receive,
            device_id=device,
            device_id_type=MESH,
        )

    unit = eye(F)
    tt[:, :N] = dnt(unit, nodes[...]).astype(BF)
    bnd[...] = dot(tt[:, :N], one_hot(brows[...], 0, N)).astype(BF)
    line[pl.ds(me, 1)] = cot[...][None]

    pl.semaphore_wait(barrier, GX - 1 + GY - 1)

    there = (me > 0, me < GX - 1, my > 0, my < GY - 1)
    halo = (
        remote(bnd, hrecv.at[1], h_s.at[1], h_r.at[1], {"gx": lax.rem(me + GX - 1, GX)}),
        remote(bnd, hrecv.at[0], h_s.at[0], h_r.at[0], {"gx": lax.rem(me + 1, GX)}),
        remote(bnd, hrecv.at[3], h_s.at[3], h_r.at[3], {"gy": lax.rem(my + GY - 1, GY)}),
        remote(bnd, hrecv.at[2], h_s.at[2], h_r.at[2], {"gy": lax.rem(my + 1, GY)}),
    )
    for k in range(4):
        pl.when(there[k])(halo[k].start)
    cots = [
        remote(
            cot,
            line.at[me],
            c_s.at[d],
            c_r.at[d],
            {"gx": lax.rem(me + d, GX)},
        )
        for d in range(1, GX)
    ]
    for copy in cots:
        copy.start()

    for i in range(2):
        for j in range(2):
            w1t[j * F : (j + 1) * F, i * F : (i + 1) * F] = dnt(
                unit, w1[i * F : (i + 1) * F, j * F : (j + 1) * F]
            ).astype(BF)
    bcol[...] = jnp.broadcast_to(
        jnp.transpose(jnp.broadcast_to(b1[...], (8, H)))[:, :1], (H, 128)
    )
    xt[2 * F :, :] = jnp.ones((16, E), BF)
    seg_ids = segs[...]
    seg_parts = jnp.concatenate(
        [
            jnp.bitwise_and(seg_ids, 255).astype(F32).astype(BF),
            jnp.right_shift(seg_ids, 8).astype(F32).astype(BF),
        ],
        axis=0,
    )

    def block(b, width=W):
        return pl.ds(pl.multiple_of(b * width, width), width)

    def gather(b, carry):
        targets = id_row(tgt, b * 8, 8)
        sources = id_row(src, b * 8, 8)
        live = id_row(mask, b * 8, 8)
        low = one_hot(jnp.bitwise_and(targets, 127), 0, 128)
        found = dot(seg_parts, low)
        found = found[:16] + 256.0 * found[16:]
        high = lax.broadcasted_iota(jnp.int32, (16, W), 0) == jnp.right_shift(targets, 7)
        segment = jnp.sum(jnp.where(high, found, 0.0), axis=0, keepdims=True)
        segment = jnp.where(live > 0, segment, -1.0).astype(jnp.int32)
        mseg[:, block(b)] = jnp.broadcast_to(segment, (8, W))
        xt[F : 2 * F, block(b)] = dot(tt[:, :N], one_hot(targets, 0, N)).astype(BF)
        xt[:F, block(b)] = dot(tt[:, :N], one_hot(sources, 0, N)).astype(BF)
        return carry

    lax.fori_loop(0, E // W, gather, 0)

    for k, coming in enumerate((halo[1], halo[0], halo[3], halo[2])):
        pl.when(there[k])(coming.wait_recv)

        @pl.when(jnp.logical_not(there[k]))
        def _(k=k):
            hrecv[k] = jnp.zeros((F, NB), BF)

        tt[:, N + k * NB : N + (k + 1) * NB] = hrecv[k]
    for copy in cots:
        copy.wait_recv()
    lines = jnp.concatenate([line[g] for g in range(GX)], axis=0)
    line_t[...] = dnt(unit, lines).astype(BF)

    def edges(b, carry):
        sources = id_row(src, b * 8, 8)
        xt[:F, block(b)] = (
            xt[:F, block(b)].astype(F32) + dot(tt[:, N:], one_hot(sources, N, HALO))
        ).astype(BF)
        chosen = one_hot(mseg[:1, block(b)], 0, SEG)
        gm = dot(line_t[...], chosen).astype(BF)
        bias = jnp.concatenate([bcol[...]] * (W // 128), axis=1)
        x = dot(w1t[...], xt[: 2 * F, block(b)]) + bias
        gh = dot(w2[...], gm)
        square = x * x
        t = jnp.tanh(x * (0.7978845608028654 + 0.035677408136300125 * square))
        half = 0.5 + 0.5 * t
        hid[:, block(b)] = (x * half).astype(BF)
        slope = half + (0.5 * x) * (1.0 - t * t) * (
            0.7978845608028654 + 0.10703222440890037 * square
        )
        gp[:, block(b)] = (gh * slope).astype(BF)
        return carry

    lax.fori_loop(0, E // W, edges, 0)

    w2v = w2[...]

    def segment_sums(b, carry):
        first = b * 256
        edge_hot = one_hot(mseg[:1, :], first, 256)
        high, low = split(dnt(edge_hot, hid[...]))
        node_hot = one_hot(id_row(segs, 0, N // 128), first, 256)
        part = dot(high, w2v) + dot(low, w2v) + dot(node_hot, nodes[...])
        for i in range(8):
            psend[b * 8 + i] = part[i * SR : (i + 1) * SR]
        lines_t = line_t[:, block(b, 256)]
        add = dot(lines_t, high) + dot(lines_t, low)
        for c in range(2):
            pwf[c, 512:768, :] = pwf[c, 512:768, :] + add[:, c * HW : (c + 1) * HW]
        return carry

    pwf[:, 512:768, :] = jnp.zeros((2, 256, HW), F32)
    lax.fori_loop(0, SEG // 256, segment_sums, 0)
    pools = [
        remote(
            psend.at[lax.rem(me + d, GX)],
            precv.at[d],
            p_s.at[d],
            p_r.at[d],
            {"gx": lax.rem(me + d, GX)},
        )
        for d in range(1, GX)
    ]
    for copy in pools:
        copy.start()

    for c in range(2):
        first = dnt(xt[...], gp[c * HW : (c + 1) * HW, :])
        pwf[c, 0:512, :] = first[:512]
        pwf[c, 768:784, :] = first[512:]
    for c in range(2):
        pws[c] = pwf[c].astype(BF)
    pair = remote(pws.at[1 - core], cbuf, core_s, core_r, {"gy": sib})
    pair.start()

    def input_grads(b, carry):
        gi[:, block(b)] = dot(w1[...], gp[:, block(b)]).astype(BF)
        return carry

    lax.fori_loop(0, E // W, input_grads, 0)

    pair.wait_recv()
    csum[...] = (pwf[core] + cbuf[...].astype(F32)).astype(BF)

    def rows_of(member):
        return pl.ds(pl.multiple_of(member * CH, 16), CH)

    scatter = []
    for d in range(1, GX):
        to = lax.rem(me + d, GX)
        scatter.append(
            remote(csum.at[rows_of(to)], rsb.at[d], rs_s.at[d], rs_r.at[d], {"gx": to})
        )
        scatter[-1].start()
    bias_rows = csum.at[pl.ds(768, 16)]
    bias_scatter = [
        remote(bias_rows, rsbias.at[d], rb_s.at[d], rb_r.at[d], {"gx": lax.rem(me + d, GX)})
        for d in range(1, GX)
    ]
    for d in range(1, GX):
        pl.when(me + d == GX)(bias_scatter[d - 1].start)

    all_src = id_row(src, 0, 32)
    slots = dnt(one_hot(all_src, N, HALO), gi[:F, :])
    for k in range(4):
        gslot[k] = slots[k * NB : (k + 1) * NB].astype(BF)
    back = (
        remote(gslot.at[0], gret.at[0], g_s.at[0], g_r.at[0], {"gx": lax.rem(me + GX - 1, GX)}),
        remote(gslot.at[1], gret.at[1], g_s.at[1], g_r.at[1], {"gx": lax.rem(me + 1, GX)}),
        remote(gslot.at[2], gret.at[2], g_s.at[2], g_r.at[2], {"gy": lax.rem(my + GY - 1, GY)}),
        remote(gslot.at[3], gret.at[3], g_s.at[3], g_r.at[3], {"gy": lax.rem(my + 1, GY)}),
    )
    for k in range(4):
        pl.when(there[k])(back[k].start)

    seg_cols = jnp.transpose(segs[...].astype(F32)).astype(jnp.int32)

    def own(b, carry):
        first = b * 512
        s = dnt(one_hot(id_row(src, 0, 32), first, 512), gi[:F, :])
        t = dnt(one_hot(id_row(tgt, 0, 32), first, 512), gi[F:, :])
        acc[block(b, 512), :] = s + t
        return carry

    lax.fori_loop(0, 2, own, 0)

    for copy in scatter:
        copy.wait_recv()
    total = csum[rows_of(me), :].astype(F32)
    for d in range(1, GX):
        total = total + rsb[d].astype(F32)
    zb[pl.ds(z, 1)] = total[None]
    over_z = []
    for d in range(1, 4):
        over_z.append(
            remote(
                zb.at[z], zb.at[z], z_s.at[d], z_r.at[d], {"gy": lax.rem(my + 2 * d, GY)}
            )
        )
        over_z[-1].start()
    bias_z = [
        remote(zbias.at[z], zbias.at[z], zb_s.at[d], zb_r.at[d], {"gy": lax.rem(my + 2 * d, GY)})
        for d in range(1, 4)
    ]

    @pl.when(me == 0)
    def _():
        for copy in bias_scatter:
            copy.wait_recv()
        sums = csum[768:784, :].astype(F32)
        for d in range(1, GX):
            sums = sums + rsbias[d].astype(F32)
        zbias[pl.ds(z, 1)] = sums[None]
        for copy in bias_z:
            copy.start()

    lax.fori_loop(2, 3, own, 0)

    for copy in over_z:
        copy.wait_recv()
    total = (zb[0] + zb[1]) + (zb[2] + zb[3])
    ag[pl.ds(core, 1), rows_of(me), :] = total.astype(BF)[None]
    gathers = []
    for d in range(1, GX):
        to = lax.rem(me + d, GX)
        place = ag.at[core, rows_of(me)]
        gathers.append(remote(place, place, ag_s.at[d], ag_r.at[d], {"gx": to}))
        gathers[-1].start()
    place = ag.at[core, rows_of(me)]
    forwards = [remote(place, place, fw_s.at[0], fw_r.at[0], {"gy": sib})]
    forwards[0].start()
    bias_place = ag.at[core, pl.ds(768, 16)]
    bias_gathers = [
        remote(
            bias_place, bias_place, agb_s.at[d], agb_r.at[d], {"gx": lax.rem(me + d, GX)}
        )
        for d in range(1, GX)
    ]

    @pl.when(me == 0)
    def _():
        for copy in bias_z:
            copy.wait_recv()
        sums = (zbias[0] + zbias[1]) + (zbias[2] + zbias[3])
        ag[pl.ds(core, 1), 768:784, :] = sums.astype(BF)[None]
        for copy in bias_gathers:
            copy.start()

    lax.fori_loop(3, 4, own, 0)

    ret = jnp.zeros((NB, F), F32)
    for k, here in enumerate((there[1], there[0], there[3], there[2])):
        pl.when(here)(back[k].wait_recv)

        @pl.when(jnp.logical_not(here))
        def _(k=k):
            gret[k] = jnp.zeros((NB, F), BF)

        ret = ret + gret[k].astype(F32)
    ret_parts = jnp.concatenate(split(ret), axis=0)
    lines = jnp.concatenate([line[g] for g in range(GX)], axis=0)
    for r in range(N // 128):
        rows = slice(r * 128, (r + 1) * 128)
        seg_hot = jnp.where(
            lax.broadcasted_iota(jnp.int32, (128, SEG), 1) == seg_cols[:, r : r + 1], 1.0, 0.0
        ).astype(BF)
        place_hot = one_hot(brows[...], r * 128, 128)
        place_hot = jnp.concatenate([place_hot, place_hot], axis=1)
        gnodes[rows, :] = (acc[rows, :] + dot(seg_hot, lines) + dot(place_hot, ret_parts)).astype(
            BF
        )

    for copy in pools:
        copy.wait_recv()
    sums = psend[me]
    for d in range(1, GX):
        sums = sums + precv[d]
    pooled[...] = sums.astype(BF)

    for d in range(1, GX):
        gathers[d - 1].wait_recv()
        place = ag.at[core, rows_of(lax.rem(me + GX - d, GX))]
        forwards.append(remote(place, place, fw_s.at[d], fw_r.at[d], {"gy": sib}))
        forwards[-1].start()

    @pl.when(me > 0)
    def _():
        for d in range(1, GX):
            pl.when(me == d)(bias_gathers[d - 1].wait_recv)

    forwards.append(remote(bias_place, bias_place, fw_s.at[GX], fw_r.at[GX], {"gy": sib}))
    forwards[-1].start()
    for copy in forwards:
        copy.wait_recv()
    gw[...] = ag[...]

    for k in range(4):
        pl.when(there[k])(halo[k].wait_send)
        pl.when(there[k])(back[k].wait_send)
    for group in (cots, pools, scatter, over_z, gathers, forwards, [pair]):
        for copy in group:
            copy.wait_send()
    for d in range(1, GX):
        pl.when(me + d == GX)(bias_scatter[d - 1].wait_send)

    @pl.when(me == 0)
    def _():
        for copy in bias_z:
            copy.wait_send()
        for copy in bias_gathers:
            copy.wait_send()


def local(nodes, brows, src, tgt, mask, segs, w1, b1, w2, cot):
    dma = pltpu.SemaphoreType.DMA
    scratch = [
        pltpu.VMEM((F, N + HALO), BF),
        pltpu.VMEM((H, 2 * F), BF),
        pltpu.VMEM((H, 128), F32),
        pltpu.VMEM((F, NB), BF),
        pltpu.VMEM((4, F, NB), BF),
        pltpu.VMEM((GX, SR, F), BF),
        pltpu.VMEM((F, SEG), BF),
        pltpu.VMEM((2 * F + 16, E), BF),
        pltpu.VMEM((8, E), jnp.int32),
        pltpu.VMEM((H, E), BF),
        pltpu.VMEM((H, E), BF),
        pltpu.VMEM((2 * F, E), BF),
        pltpu.VMEM((2, PW, HW), F32),
        pltpu.VMEM((2, PW, HW), BF),
        pltpu.VMEM((PW, HW), BF),
        pltpu.VMEM((PW, HW), BF),
        pltpu.VMEM((GX, CH, HW), BF),
        pltpu.VMEM((GX, 16, HW), BF),
        pltpu.VMEM((4, CH, HW), F32),
        pltpu.VMEM((4, 16, HW), F32),
        pltpu.VMEM((2, PW, HW), BF),
        pltpu.VMEM((GX, SR, F), F32),
        pltpu.VMEM((GX, SR, F), F32),
        pltpu.VMEM((4, NB, F), BF),
        pltpu.VMEM((4, NB, F), BF),
        pltpu.VMEM((N, F), F32),
        dma((4,)),
        dma((4,)),
        dma((GX,)),
        dma((GX,)),
        dma((GX,)),
        dma((GX,)),
        dma((4,)),
        dma((4,)),
        dma,
        dma,
        dma((GX,)),
        dma((GX,)),
        dma((GX,)),
        dma((GX,)),
        dma((4,)),
        dma((4,)),
        dma((4,)),
        dma((4,)),
        dma((GX,)),
        dma((GX,)),
        dma((GX,)),
        dma((GX,)),
        dma((GX + 1,)),
        dma((GX + 1,)),
    ]
    vmem = pl.BlockSpec(memory_space=pltpu.VMEM)
    pooled, gnodes, gw = pl.pallas_call(
        kernel,
        out_shape=(
            jax.ShapeDtypeStruct((SR, F), BF),
            jax.ShapeDtypeStruct((N, F), BF),
            jax.ShapeDtypeStruct((2, PW, HW), BF),
        ),
        in_specs=[vmem] * 10,
        out_specs=(vmem,) * 3,
        scratch_shapes=scratch,
        compiler_params=pltpu.CompilerParams(
            collective_id=0, has_side_effects=True, vmem_limit_bytes=60 * 2**20
        ),
    )(
        nodes,
        brows.reshape(1, NB),
        src,
        tgt,
        mask,
        segs.reshape(N // 128, 128),
        w1,
        b1.reshape(1, H),
        w2,
        cot,
    )
    scale = 1.0 / jnp.sqrt(jnp.float32(E * GX * GY))
    both = jnp.concatenate([gw[0], gw[1]], axis=1).astype(F32) * scale
    return pooled, gnodes, both[:512], both[768], both[512:768].T


def solution(mesh):
    in_specs = (
        P(("gx", "gy"), None),
        P(("gx", "gy")),
        P(("gx", "gy"), None),
        P(("gx", "gy"), None),
        P(("gx", "gy"), None),
        P(("gx", "gy")),
        P(),
        P(),
        P(),
        P(("gx", "gy"), None),
    )
    out_specs = (P(("gx", "gy"), None), P(("gx", "gy"), None), P(), P(), P())
    return jax.shard_map(local, mesh=mesh, in_specs=in_specs, out_specs=out_specs, check_vma=False)
```

time: 398 us -> 71.4 us (0.18)
  matrix products: 111 us -> 0 us
  blocking collectives: 87.2 us -> 0 us
  local copies, waits for them, and re-layouts: 79 us -> 5.41 us
  Pallas kernels: 0 us -> 65 us
  waiting for transfers between devices: 64.4 us -> 0 us
  starting transfers between devices: 28.1 us -> 0 us
  between operations: 15.8 us -> 0.68 us
  other arithmetic: 9.22 us -> 0.22 us
    dot_general x33 -> x0, matrix products: 111 us -> none  [the longest x8 34.8 us: incoming_step(): lax.dot_general(chosen, messages_block, contract_rows, preferred_element_...]
    psum x1 -> x0, blocking collectives: 65.8 us -> none  [local(): lax.psum((grad_first, grad_bias, grad_second), ('gx', 'gy'))]
    pallas_call x0 -> x1, Pallas kernels: none -> 65 us  [local(): pl.pallas_call(kernel, out_shape=(jax.ShapeDtypeStruct((SR, F), BF), jax....]
    gather x4 -> x0, local copies, waits for them, and re-layouts: 54 us -> none  [the longest x2 34.1 us: local(): inputs = jnp.concatenate([row_table[source_ids], row_table[target_ids]], 1)]
    psum x1 -> x0, waiting for transfers between devices: 40.7 us -> none  [local(): lax.psum((grad_first, grad_bias, grad_second), ('gx', 'gy'))]
    ppermute x8 -> x0, starting transfers between devices: 28 us -> none  [the longest x2 13.8 us: with_halo(): lax.ppermute(lax.slice_in_dim(block, block.shape[dim] - width, None, axis...]
    all_gather x1 -> x0, blocking collectives: 21.5 us -> none  [local(): line_rows = lax.all_gather(cotangent, 'gx', axis=0, tiled=True)]
    reduce_scatter x1 -> x0, waiting for transfers between devices: 18.8 us -> none  [local(): lax.psum_scatter(partial_sums, 'gx', scatter_dimension=0, tiled=True)]
  transfers between devices with their start and end apart: 10 -> 0, of which waited for: 4 -> 0; matrix products, arithmetic and copies ran while one was open for 18% -> 0% of each run, Pallas kernels for 0% -> 0%
where the time goes in v1:
time: 71.4 us; the launch traced here: 71.3 us
  Pallas kernels  65 us (91%)
  local copies, waits for them, and re-layouts  5.41 us (8%)
    pallas_call x1, Pallas kernels, local(): pl.pallas_call(kernel, out_shape=(jax.ShapeDtypeStruct((SR, F), BF), jax....  65 us
    unnamed x7, local copies, waits for them, and re-layouts  2.58 us
    slice x2, local copies, waits for them, and re-layouts, local(): return (pooled, gnodes, both[:512], both[768], both[512:768].T)  1.63 us

profile of v1, /device:TPU:1, one launch (start us, length us, event | category | flops | bytes accessed | tf_op | source)
XLA Modules:
  0.0 71.3 jit_solution(5756654607494171175)
XLA Ops:
  0.6 65.0 %shard_map.137 = (bf16[32,256]{1,0:T(8,128)(2,1)}, bf16[2048,256]{1,0:T(8,128)(2,1)}, bf16[2,784,256]{2,1,0:T(8,128)(2,1)}) custom-call(bf16[2048,256]{1,0:T(8,128)(2,1)} %nodes.1, s32[1,128]{1,0:T(1,128)} %bitcast.13, s32[32,128]{1,0:T(8,128)} %src.1, s32[32,128]{1,0:T(8,128)} %tgt.1, s32[32,128]{1,0:T(8,128)} %mask.1, s32[16,128]{1,0:T(8,128)} %bitcast.10, ...), custom_call_target="tpu_custom_call" | custom-call | tf_op jit(solution)/shard_map/pallas_call | solution.py:524
  65.6 1.2 %slice_bitcast_fusion.2 = (bf16[784,256]{1,0:T(8,128)(2,1)S(1)}, bf16[784,256]{1,0:T(8,128)(2,1)S(1)}) fusion(bf16[2,784,256]{2,1,0:T(8,128)(2,1)} %get-tuple-element.10), kind=kLoop, calls=%fused_computation.3 | loop fusion | bytes 1605632 | tf_op jit(solution)/shard_map/squeeze | solution.py:550
  66.8 0.2 convert_multiply_fusion
  67.0 0.6 slice.21
  67.6 0.0 copy-start.1
  67.7 0.0 copy-start
  67.7 1.0 %slice.20 = f32[512,512]{1,0:T(8,128)} slice(f32[784,512]{1,0:T(8,128)S(1)} %convert_multiply_fusion), slice={[0:512], [0:512]} | slice | bytes 2097152 | tf_op jit(solution)/shard_map/slice | solution.py:551
  68.7 1.0 %copy.15 = f32[512,256]{1,0:T(8,128)} copy(f32[512,256]{0,1:T(8,128)S(1)} %slice_bitcast_fusion) | data formatting | bytes 1048576
  69.7 0.0 copy-done.1
  69.7 0.6 copy.18
  70.3 0.0 copy-done
  70.3 1.0 %copy.19 = bf16[2048,256]{1,0:T(8,128)(2,1)} copy(bf16[2048,256]{1,0:T(8,128)(2,1)S(1)} %copy-done) | data formatting | bytes 2097152
  (1 shorter events, 0.0 us)
Async XLA Ops:
  67.6 2.1 %copy-start.1 = (bf16[32,256]{1,0:T(8,128)(2,1)S(1)}, bf16[32,256]{1,0:T(8,128)(2,1)}, u32[]{:S(2)}) copy-start(bf16[32,256]{1,0:T(8,128)(2,1)} %get-tuple-element.23) | copy-start | bytes 49156
  67.7 2.7 %copy-start = (bf16[2048,256]{1,0:T(8,128)(2,1)S(1)}, bf16[2048,256]{1,0:T(8,128)(2,1)}, u32[]{:S(2)}) copy-start(bf16[2048,256]{1,0:T(8,128)(2,1)} %get-tuple-element.24) | copy-start | bytes 3145732

commit v2 on v1

--- a/solution.py
+++ b/solution.py
@@ -21,7 +21,6 @@
 GX = 16
 GY = 8
 W = 1024
-CH = 48
 PW = 784
 HW = H // 2
 NT = (((1,), (1,)), ((), ()))
@@ -56,6 +55,19 @@
 
 
 def kernel(
+    nodes_h,
+    brows_h,
+    src_h,
+    tgt_h,
+    mask_h,
+    segs_h,
+    w1_h,
+    b1_h,
+    w2_h,
+    cot_h,
+    pooled_h,
+    gnodes_h,
+    gw_h,
     nodes,
     brows,
     src,
@@ -68,7 +80,6 @@
     cot,
     pooled,
     gnodes,
-    gw,
     tt,
     w1t,
     bcol,
@@ -85,9 +96,11 @@
     pws,
     cbuf,
     csum,
-    rsb,
+    rsb_a,
+    rsb_b,
     rsbias,
-    zb,
+    zb_a,
+    zb_b,
     zbias,
     ag,
     psend,
@@ -95,6 +108,8 @@
     gslot,
     gret,
     acc,
+    in_s,
+    out_s,
     h_s,
     h_r,
     c_s,
@@ -146,7 +161,25 @@
             device_id_type=MESH,
         )
 
+    pairs = (
+        (nodes_h, nodes),
+        (brows_h, brows),
+        (cot_h, cot),
+        (w1_h, w1),
+        (b1_h, b1),
+        (segs_h, segs),
+        (tgt_h, tgt),
+        (src_h, src),
+        (mask_h, mask),
+        (w2_h, w2),
+    )
+    loads = [pltpu.make_async_copy(a, b, in_s.at[i]) for i, (a, b) in enumerate(pairs)]
+    for copy in loads:
+        copy.start()
+
     unit = eye(F)
+    for copy in loads[:3]:
+        copy.wait()
     tt[:, :N] = dnt(unit, nodes[...]).astype(BF)
     bnd[...] = dot(tt[:, :N], one_hot(brows[...], 0, N)).astype(BF)
     line[pl.ds(me, 1)] = cot[...][None]
@@ -174,6 +207,8 @@
     ]
     for copy in cots:
         copy.start()
+    for copy in loads[3:]:
+        copy.wait()
 
     for i in range(2):
         for j in range(2):
@@ -248,6 +283,152 @@
 
     lax.fori_loop(0, E // W, edges, 0)
 
+    firsts, counts = (0, 528), (528, 256)
+    shares = (32, 16)
+    arrived = (rsb_a, rsb_b)
+    by_z = (zb_a, zb_b)
+
+    def rows_of(part, member):
+        return pl.ds(pl.multiple_of(firsts[part] + member * shares[part], 16), shares[part])
+
+    def whole(part):
+        return pl.ds(firsts[part], counts[part])
+
+    peers = [lax.rem(me + d, GX) for d in range(GX)]
+    pair, scatter, over_z, gathers, forwards = [], [], [], [], []
+    for part in range(2):
+        pair.append(
+            remote(
+                pws.at[1 - core, whole(part)],
+                cbuf.at[whole(part)],
+                core_s.at[part],
+                core_r.at[part],
+                {"gy": sib},
+            )
+        )
+        scatter.append(
+            [
+                remote(
+                    csum.at[rows_of(part, peers[d])],
+                    arrived[part].at[d],
+                    rs_s.at[part, d],
+                    rs_r.at[part, d],
+                    {"gx": peers[d]},
+                )
+                for d in range(1, GX)
+            ]
+        )
+        over_z.append(
+            [
+                remote(
+                    by_z[part].at[z],
+                    by_z[part].at[z],
+                    z_s.at[part, d],
+                    z_r.at[part, d],
+                    {"gy": lax.rem(my + 2 * d, GY)},
+                )
+                for d in range(1, 4)
+            ]
+        )
+        place = ag.at[core, rows_of(part, me)]
+        gathers.append(
+            [
+                remote(place, place, ag_s.at[part, d], ag_r.at[part, d], {"gx": peers[d]})
+                for d in range(1, GX)
+            ]
+        )
+        ways = []
+        for d in range(GX):
+            place = ag.at[core, rows_of(part, lax.rem(me + GX - d, GX))]
+            ways.append(remote(place, place, fw_s.at[part, d], fw_r.at[part, d], {"gy": sib}))
+        forwards.append(ways)
+    bias_rows = csum.at[pl.ds(512, 16)]
+    bias_scatter = [
+        remote(bias_rows, rsbias.at[d], rb_s.at[d], rb_r.at[d], {"gx": peers[d]})
+        for d in range(1, GX)
+    ]
+    bias_z = [
+        remote(zbias.at[z], zbias.at[z], zb_s.at[d], zb_r.at[d], {"gy": lax.rem(my + 2 * d, GY)})
+        for d in range(1, 4)
+    ]
+    bias_place = ag.at[core, pl.ds(512, 16)]
+    bias_gathers = [
+        remote(bias_place, bias_place, agb_s.at[d], agb_r.at[d], {"gx": peers[d]})
+        for d in range(1, GX)
+    ]
+    bias_forward = remote(bias_place, bias_place, fw_s.at[0, GX], fw_r.at[0, GX], {"gy": sib})
+
+    def to_pair(part):
+        pws[:, whole(part), :] = pwf[:, whole(part), :].astype(BF)
+        pair[part].start()
+
+    def to_members(part):
+        pair[part].wait_recv()
+        csum[whole(part), :] = (
+            pwf[core, whole(part), :] + cbuf[whole(part), :].astype(F32)
+        ).astype(BF)
+        for copy in scatter[part]:
+            copy.start()
+        if part == 0:
+            for d in range(1, GX):
+                pl.when(me + d == GX)(bias_scatter[d - 1].start)
+
+    def to_z(part):
+        for copy in scatter[part]:
+            copy.wait_recv()
+        total = csum[rows_of(part, me), :].astype(F32)
+        for d in range(1, GX):
+            total = total + arrived[part][d].astype(F32)
+        by_z[part][pl.ds(z, 1)] = total[None]
+        for copy in over_z[part]:
+            copy.start()
+        if part == 0:
+
+            @pl.when(me == 0)
+            def _():
+                for copy in bias_scatter:
+                    copy.wait_recv()
+                sums = csum[512:528, :].astype(F32)
+                for d in range(1, GX):
+                    sums = sums + rsbias[d].astype(F32)
+                zbias[pl.ds(z, 1)] = sums[None]
+                for copy in bias_z:
+                    copy.start()
+
+    def to_all(part):
+        for copy in over_z[part]:
+            copy.wait_recv()
+        sums = by_z[part]
+        total = (sums[0] + sums[1]) + (sums[2] + sums[3])
+        ag[pl.ds(core, 1), rows_of(part, me), :] = total.astype(BF)[None]
+        for copy in gathers[part]:
+            copy.start()
+        forwards[part][0].start()
+        if part == 0:
+
+            @pl.when(me == 0)
+            def _():
+                for copy in bias_z:
+                    copy.wait_recv()
+                sums = (zbias[0] + zbias[1]) + (zbias[2] + zbias[3])
+                ag[pl.ds(core, 1), 512:528, :] = sums.astype(BF)[None]
+                for copy in bias_gathers:
+                    copy.start()
+
+    def to_other_core(part):
+        for d in range(1, GX):
+            gathers[part][d - 1].wait_recv()
+            forwards[part][d].start()
+        if part == 0:
+            for d in range(1, GX):
+                pl.when(me == d)(bias_gathers[d - 1].wait_recv)
+            bias_forward.start()
+
+    for c in range(2):
+        first = dnt(xt[...], gp[c * HW : (c + 1) * HW, :])
+        pwf[c, 0:528, :] = first
+    to_pair(0)
+
     w2v = w2[...]
 
     def segment_sums(b, carry):
@@ -261,59 +442,33 @@
         lines_t = line_t[:, block(b, 256)]
         add = dot(lines_t, high) + dot(lines_t, low)
         for c in range(2):
-            pwf[c, 512:768, :] = pwf[c, 512:768, :] + add[:, c * HW : (c + 1) * HW]
+            pwf[c, 528:784, :] = pwf[c, 528:784, :] + add[:, c * HW : (c + 1) * HW]
+        pl.when(b == 0)(functools.partial(to_members, 0))
         return carry
 
-    pwf[:, 512:768, :] = jnp.zeros((2, 256, HW), F32)
+    pwf[:, 528:784, :] = jnp.zeros((2, 256, HW), F32)
     lax.fori_loop(0, SEG // 256, segment_sums, 0)
+    to_pair(1)
     pools = [
         remote(
-            psend.at[lax.rem(me + d, GX)],
+            psend.at[peers[d]],
             precv.at[d],
             p_s.at[d],
             p_r.at[d],
-            {"gx": lax.rem(me + d, GX)},
+            {"gx": peers[d]},
         )
         for d in range(1, GX)
     ]
     for copy in pools:
         copy.start()
 
-    for c in range(2):
-        first = dnt(xt[...], gp[c * HW : (c + 1) * HW, :])
-        pwf[c, 0:512, :] = first[:512]
-        pwf[c, 768:784, :] = first[512:]
-    for c in range(2):
-        pws[c] = pwf[c].astype(BF)
-    pair = remote(pws.at[1 - core], cbuf, core_s, core_r, {"gy": sib})
-    pair.start()
-
     def input_grads(b, carry):
         gi[:, block(b)] = dot(w1[...], gp[:, block(b)]).astype(BF)
         return carry
 
     lax.fori_loop(0, E // W, input_grads, 0)
-
-    pair.wait_recv()
-    csum[...] = (pwf[core] + cbuf[...].astype(F32)).astype(BF)
-
-    def rows_of(member):
-        return pl.ds(pl.multiple_of(member * CH, 16), CH)
-
-    scatter = []
-    for d in range(1, GX):
-        to = lax.rem(me + d, GX)
-        scatter.append(
-            remote(csum.at[rows_of(to)], rsb.at[d], rs_s.at[d], rs_r.at[d], {"gx": to})
-        )
-        scatter[-1].start()
-    bias_rows = csum.at[pl.ds(768, 16)]
-    bias_scatter = [
-        remote(bias_rows, rsbias.at[d], rb_s.at[d], rb_r.at[d], {"gx": lax.rem(me + d, GX)})
-        for d in range(1, GX)
-    ]
-    for d in range(1, GX):
-        pl.when(me + d == GX)(bias_scatter[d - 1].start)
+    to_members(1)
+    to_z(0)
 
     all_src = id_row(src, 0, 32)
     slots = dnt(one_hot(all_src, N, HALO), gi[:F, :])
@@ -328,80 +483,23 @@
     for k in range(4):
         pl.when(there[k])(back[k].start)
 
-    seg_cols = jnp.transpose(segs[...].astype(F32)).astype(jnp.int32)
-
     def own(b, carry):
         first = b * 512
         s = dnt(one_hot(id_row(src, 0, 32), first, 512), gi[:F, :])
         t = dnt(one_hot(id_row(tgt, 0, 32), first, 512), gi[F:, :])
         acc[block(b, 512), :] = s + t
+
+        @pl.when(b == 0)
+        def _():
+            to_z(1)
+            to_all(0)
+
+        pl.when(b == 1)(functools.partial(to_all, 1))
+        pl.when(b == 2)(functools.partial(to_other_core, 0))
+        pl.when(b == 3)(functools.partial(to_other_core, 1))
         return carry
 
-    lax.fori_loop(0, 2, own, 0)
-
-    for copy in scatter:
-        copy.wait_recv()
-    total = csum[rows_of(me), :].astype(F32)
-    for d in range(1, GX):
-        total = total + rsb[d].astype(F32)
-    zb[pl.ds(z, 1)] = total[None]
-    over_z = []
-    for d in range(1, 4):
-        over_z.append(
-            remote(
-                zb.at[z], zb.at[z], z_s.at[d], z_r.at[d], {"gy": lax.rem(my + 2 * d, GY)}
-            )
-        )
-        over_z[-1].start()
-    bias_z = [
-        remote(zbias.at[z], zbias.at[z], zb_s.at[d], zb_r.at[d], {"gy": lax.rem(my + 2 * d, GY)})
-        for d in range(1, 4)
-    ]
-
-    @pl.when(me == 0)
-    def _():
-        for copy in bias_scatter:
-            copy.wait_recv()
-        sums = csum[768:784, :].astype(F32)
-        for d in range(1, GX):
-            sums = sums + rsbias[d].astype(F32)
-        zbias[pl.ds(z, 1)] = sums[None]
-        for copy in bias_z:
-            copy.start()
-
-    lax.fori_loop(2, 3, own, 0)
-
-    for copy in over_z:
-        copy.wait_recv()
-    total = (zb[0] + zb[1]) + (zb[2] + zb[3])
-    ag[pl.ds(core, 1), rows_of(me), :] = total.astype(BF)[None]
-    gathers = []
-    for d in range(1, GX):
-        to = lax.rem(me + d, GX)
-        place = ag.at[core, rows_of(me)]
-        gathers.append(remote(place, place, ag_s.at[d], ag_r.at[d], {"gx": to}))
-        gathers[-1].start()
-    place = ag.at[core, rows_of(me)]
-    forwards = [remote(place, place, fw_s.at[0], fw_r.at[0], {"gy": sib})]
-    forwards[0].start()
-    bias_place = ag.at[core, pl.ds(768, 16)]
-    bias_gathers = [
-        remote(
-            bias_place, bias_place, agb_s.at[d], agb_r.at[d], {"gx": lax.rem(me + d, GX)}
-        )
-        for d in range(1, GX)
-    ]
-
-    @pl.when(me == 0)
-    def _():
-        for copy in bias_z:
-            copy.wait_recv()
-        sums = (zbias[0] + zbias[1]) + (zbias[2] + zbias[3])
-        ag[pl.ds(core, 1), 768:784, :] = sums.astype(BF)[None]
-        for copy in bias_gathers:
-            copy.start()
-
-    lax.fori_loop(3, 4, own, 0)
+    lax.fori_loop(0, N // 512, own, 0)
 
     ret = jnp.zeros((NB, F), F32)
     for k, here in enumerate((there[1], there[0], there[3], there[2])):
@@ -414,6 +512,8 @@
         ret = ret + gret[k].astype(F32)
     ret_parts = jnp.concatenate(split(ret), axis=0)
     lines = jnp.concatenate([line[g] for g in range(GX)], axis=0)
+    seg_cols = jnp.transpose(segs[...].astype(F32)).astype(jnp.int32)
+    stores = []
     for r in range(N // 128):
         rows = slice(r * 128, (r + 1) * 128)
         seg_hot = jnp.where(
@@ -424,6 +524,12 @@
         gnodes[rows, :] = (acc[rows, :] + dot(seg_hot, lines) + dot(place_hot, ret_parts)).astype(
             BF
         )
+        if r % 4 == 3:
+            done = pl.ds((r - 3) * 128, 512)
+            stores.append(
+                pltpu.make_async_copy(gnodes.at[done], gnodes_h.at[done], out_s.at[r // 4])
+            )
+            stores[-1].start()
 
     for copy in pools:
         copy.wait_recv()
@@ -431,28 +537,20 @@
     for d in range(1, GX):
         sums = sums + precv[d]
     pooled[...] = sums.astype(BF)
-
-    for d in range(1, GX):
-        gathers[d - 1].wait_recv()
-        place = ag.at[core, rows_of(lax.rem(me + GX - d, GX))]
-        forwards.append(remote(place, place, fw_s.at[d], fw_r.at[d], {"gy": sib}))
-        forwards[-1].start()
-
-    @pl.when(me > 0)
-    def _():
-        for d in range(1, GX):
-            pl.when(me == d)(bias_gathers[d - 1].wait_recv)
-
-    forwards.append(remote(bias_place, bias_place, fw_s.at[GX], fw_r.at[GX], {"gy": sib}))
-    forwards[-1].start()
-    for copy in forwards:
-        copy.wait_recv()
-    gw[...] = ag[...]
+    stores.append(pltpu.make_async_copy(pooled, pooled_h, out_s.at[4]))
+    stores[-1].start()
+
+    for part in range(2):
+        for copy in forwards[part]:
+            copy.wait_recv()
+    bias_forward.wait_recv()
+    stores.append(pltpu.make_async_copy(ag, gw_h, out_s.at[5]))
+    stores[-1].start()
 
     for k in range(4):
         pl.when(there[k])(halo[k].wait_send)
         pl.when(there[k])(back[k].wait_send)
-    for group in (cots, pools, scatter, over_z, gathers, forwards, [pair]):
+    for group in (cots, pools, pair, [bias_forward], *scatter, *over_z, *gathers, *forwards):
         for copy in group:
             copy.wait_send()
     for d in range(1, GX):
@@ -465,76 +563,33 @@
         for copy in bias_gathers:
             copy.wait_send()
 
+    for copy in stores:
+        copy.wait()
+
+
+def finish(scale, pooled, gnodes, gw, pooled_o, gnodes_o, first_o, bias_o, second_o, buf, sems):
+    moves = [
+        pltpu.make_async_copy(gw, buf, sems.at[0]),
+        pltpu.make_async_copy(gnodes, gnodes_o, sems.at[1]),
+        pltpu.make_async_copy(pooled, pooled_o, sems.at[2]),
+    ]
+    for copy in moves:
+        copy.start()
+    moves[0].wait()
+    unit = eye(HW)
+    for c in range(2):
+        half = slice(c * HW, (c + 1) * HW)
+        first_o[:, half] = buf[c, 0:512, :].astype(F32) * scale
+        bias_o[:, half] = buf[c, 512:528, :].astype(F32)[:1] * scale
+        second_o[half, :] = dnt(unit, buf[c, 528:784, :]) * scale
+    moves[1].wait()
+    moves[2].wait()
+
 
 def local(nodes, brows, src, tgt, mask, segs, w1, b1, w2, cot):
     dma = pltpu.SemaphoreType.DMA
-    scratch = [
-        pltpu.VMEM((F, N + HALO), BF),
-        pltpu.VMEM((H, 2 * F), BF),
-        pltpu.VMEM((H, 128), F32),
-        pltpu.VMEM((F, NB), BF),
-        pltpu.VMEM((4, F, NB), BF),
-        pltpu.VMEM((GX, SR, F), BF),
-        pltpu.VMEM((F, SEG), BF),
-        pltpu.VMEM((2 * F + 16, E), BF),
-        pltpu.VMEM((8, E), jnp.int32),
-        pltpu.VMEM((H, E), BF),
-        pltpu.VMEM((H, E), BF),
-        pltpu.VMEM((2 * F, E), BF),
-        pltpu.VMEM((2, PW, HW), F32),
-        pltpu.VMEM((2, PW, HW), BF),
-        pltpu.VMEM((PW, HW), BF),
-        pltpu.VMEM((PW, HW), BF),
-        pltpu.VMEM((GX, CH, HW), BF),
-        pltpu.VMEM((GX, 16, HW), BF),
-        pltpu.VMEM((4, CH, HW), F32),
-        pltpu.VMEM((4, 16, HW), F32),
-        pltpu.VMEM((2, PW, HW), BF),
-        pltpu.VMEM((GX, SR, F), F32),
-        pltpu.VMEM((GX, SR, F), F32),
-        pltpu.VMEM((4, NB, F), BF),
-        pltpu.VMEM((4, NB, F), BF),
-        pltpu.VMEM((N, F), F32),
-        dma((4,)),
-        dma((4,)),
-        dma((GX,)),
-        dma((GX,)),
-        dma((GX,)),
-        dma((GX,)),
-        dma((4,)),
-        dma((4,)),
-        dma,
-        dma,
-        dma((GX,)),
-        dma((GX,)),
-        dma((GX,)),
-        dma((GX,)),
-        dma((4,)),
-        dma((4,)),
-        dma((4,)),
-        dma((4,)),
-        dma((GX,)),
-        dma((GX,)),
-        dma((GX,)),
-        dma((GX,)),
-        dma((GX + 1,)),
-        dma((GX + 1,)),
-    ]
-    vmem = pl.BlockSpec(memory_space=pltpu.VMEM)
-    pooled, gnodes, gw = pl.pallas_call(
-        kernel,
-        out_shape=(
-            jax.ShapeDtypeStruct((SR, F), BF),
-            jax.ShapeDtypeStruct((N, F), BF),
-            jax.ShapeDtypeStruct((2, PW, HW), BF),
-        ),
-        in_specs=[vmem] * 10,
-        out_specs=(vmem,) * 3,
-        scratch_shapes=scratch,
-        compiler_params=pltpu.CompilerParams(
-            collective_id=0, has_side_effects=True, vmem_limit_bytes=60 * 2**20
-        ),
-    )(
+    int32 = jnp.int32
+    arguments = (
         nodes,
         brows.reshape(1, NB),
         src,
@@ -546,9 +601,86 @@
         w2,
         cot,
     )
-    scale = 1.0 / jnp.sqrt(jnp.float32(E * GX * GY))
-    both = jnp.concatenate([gw[0], gw[1]], axis=1).astype(F32) * scale
-    return pooled, gnodes, both[:512], both[768], both[512:768].T
+    scratch = [pltpu.VMEM(a.shape, a.dtype) for a in arguments]
+    scratch += [
+        pltpu.VMEM((SR, F), BF),
+        pltpu.VMEM((N, F), BF),
+        pltpu.VMEM((F, N + HALO), BF),
+        pltpu.VMEM((H, 2 * F), BF),
+        pltpu.VMEM((H, 128), F32),
+        pltpu.VMEM((F, NB), BF),
+        pltpu.VMEM((4, F, NB), BF),
+        pltpu.VMEM((GX, SR, F), BF),
+        pltpu.VMEM((F, SEG), BF),
+        pltpu.VMEM((2 * F + 16, E), BF),
+        pltpu.VMEM((8, E), int32),
+        pltpu.VMEM((H, E), BF),
+        pltpu.VMEM((H, E), BF),
+        pltpu.VMEM((2 * F, E), BF),
+        pltpu.VMEM((2, PW, HW), F32),
+        pltpu.VMEM((2, PW, HW), BF),
+        pltpu.VMEM((PW, HW), BF),
+        pltpu.VMEM((PW, HW), BF),
+        pltpu.VMEM((GX, 32, HW), BF),
+        pltpu.VMEM((GX, 16, HW), BF),
+        pltpu.VMEM((GX, 16, HW), BF),
+        pltpu.VMEM((4, 32, HW), F32),
+        pltpu.VMEM((4, 16, HW), F32),
+        pltpu.VMEM((4, 16, HW), F32),
+        pltpu.VMEM((2, PW, HW), BF),
+        pltpu.VMEM((GX, SR, F), F32),
+        pltpu.VMEM((GX, SR, F), F32),
+        pltpu.VMEM((4, NB, F), BF),
+        pltpu.VMEM((4, NB, F), BF),
+        pltpu.VMEM((N, F), F32),
+        dma((10,)),
+        dma((6,)),
+    ]
+    for shape in (
+        (4,),
+        (GX,),
+        (GX,),
+        (4,),
+        (2,),
+        (2, GX),
+        (GX,),
+        (2, 4),
+        (4,),
+        (2, GX),
+        (GX,),
+        (2, GX + 1),
+    ):
+        scratch += [dma(shape), dma(shape)]
+    anywhere = pl.BlockSpec(memory_space=pl.ANY)
+    vmem = pl.BlockSpec(memory_space=pltpu.VMEM)
+    outs = (
+        jax.ShapeDtypeStruct((SR, F), BF),
+        jax.ShapeDtypeStruct((N, F), BF),
+    )
+    pooled, gnodes, gw = pl.pallas_call(
+        kernel,
+        out_shape=(*outs, jax.ShapeDtypeStruct((2, PW, HW), BF)),
+        in_specs=[anywhere] * 10,
+        out_specs=(anywhere,) * 3,
+        scratch_shapes=scratch,
+        compiler_params=pltpu.CompilerParams(
+            collective_id=0, has_side_effects=True, vmem_limit_bytes=60 * 2**20
+        ),
+    )(*arguments)
+    pooled, gnodes, first, bias, second = pl.pallas_call(
+        functools.partial(finish, float((E * GX * GY) ** -0.5)),
+        out_shape=(
+            *outs,
+            jax.ShapeDtypeStruct((H, H), F32),
+            jax.ShapeDtypeStruct((1, H), F32),
+            jax.ShapeDtypeStruct((H, F), F32),
+        ),
+        in_specs=[anywhere] * 3,
+        out_specs=(anywhere, anywhere, vmem, vmem, vmem),
+        scratch_shapes=[pltpu.VMEM((2, PW, HW), BF), dma((3,))],
+        compiler_params=pltpu.CompilerParams(vmem_limit_bytes=16 * 2**20),
+    )(pooled, gnodes, gw)
+    return pooled, gnodes, first, bias.reshape(H), second
 
 
 def solution(mesh):

time: 71.4 us -> 68.7 us (0.962)
  local copies, waits for them, and re-layouts: 5.41 us -> 3.07 us
    slice x2 -> x0, local copies, waits for them, and re-layouts: 1.63 us -> none  [local(): return (pooled, gnodes, both[:512], both[768], both[512:768].T)]
    squeeze x1 -> x0, local copies, waits for them, and re-layouts: 1.17 us -> none  [local(): both = jnp.concatenate([gw[0], gw[1]], axis=1).astype(F32) * scale]
    unnamed x7 -> x6, local copies, waits for them, and re-layouts: 2.58 us -> 3.07 us
    pallas_call x1 -> x2, Pallas kernels: 65 us -> 64.5 us  [the longest x1 62.3 us: local(): pl.pallas_call(kernel, out_shape=(*outs, jax.ShapeDtypeStruct((2, PW, HW)...]
where the time goes in v2:
time: 68.7 us; the launch traced here: 68.4 us
  Pallas kernels  64.5 us (94%)
  local copies, waits for them, and re-layouts  3.07 us (4%)
  between operations  0.81 us (1%)
    pallas_call x1, Pallas kernels, local(): pl.pallas_call(kernel, out_shape=(*outs, jax.ShapeDtypeStruct((2, PW, HW)...  62.3 us
    unnamed x6, local copies, waits for them, and re-layouts  3.07 us
    pallas_call x1, Pallas kernels, local(): pl.pallas_call(functools.partial(finish, float((E * GX * GY) ** (-0.5))),...  2.21 us

profile of v2, /device:TPU:1, one launch (start us, length us, event | category | flops | bytes accessed | tf_op | source)
XLA Modules:
  0.0 68.4 jit_solution(211826567248974422)
XLA Ops:
  0.6 62.3 %shard_map.137 = (bf16[32,256]{1,0:T(8,128)(2,1)}, bf16[2048,256]{1,0:T(8,128)(2,1)}, bf16[2,784,256]{2,1,0:T(8,128)(2,1)}) custom-call(bf16[2048,256]{1,0:T(8,128)(2,1)} %nodes_h.1, s32[1,128]{1,0:T(1,128)} %bitcast.6, s32[32,128]{1,0:T(8,128)} %src_h.1, s32[32,128]{1,0:T(8,128)} %tgt_h.1, s32[32,128]{1,0:T(8,128)} %mask_h.1, s32[16,128]{1,0:T(8,128)} %bitcast.4, ...), custom_call_target="tpu_custom_call" | custom-call | tf_op jit(solution)/shard_map/pallas_call | solution.py:660
  63.0 0.0 copy-start
  63.0 1.2 %copy-done = bf16[2048,256]{1,0:T(8,128)(2,1)S(1)} copy-done((bf16[2048,256]{1,0:T(8,128)(2,1)S(1)}, bf16[2048,256]{1,0:T(8,128)(2,1)}, u32[]{:S(2)}) %copy-start) | copy-done | bytes 1048600
  64.2 0.0 copy-start.1
  64.2 1.1 %copy-done.1 = bf16[2,784,256]{2,1,0:T(8,128)(2,1)S(1)} copy-done((bf16[2,784,256]{2,1,0:T(8,128)(2,1)S(1)}, bf16[2,784,256]{2,1,0:T(8,128)(2,1)}, u32[]{:S(2)}) %copy-start.1) | copy-done | bytes 802840
  65.3 0.0 copy-start.2
  65.3 0.7 %copy-done.2 = bf16[32,256]{1,0:T(8,128)(2,1)S(1)} copy-done((bf16[32,256]{1,0:T(8,128)(2,1)S(1)}, bf16[32,256]{1,0:T(8,128)(2,1)}, u32[]{:S(2)}) %copy-start.2) | copy-done | bytes 16408
  66.0 2.2 %shard_map.138 = (bf16[32,256]{1,0:T(8,128)(2,1)}, bf16[2048,256]{1,0:T(8,128)(2,1)}, f32[512,512]{1,0:T(8,128)}, f32[1,512]{1,0:T(1,128)}, f32[512,256]{1,0:T(8,128)}) custom-call(bf16[32,256]{1,0:T(8,128)(2,1)S(1)} %copy-done.2, bf16[2048,256]{1,0:T(8,128)(2,1)S(1)} %copy-done, bf16[2,784,256]{2,1,0:T(8,128)(2,1)S(1)} %copy-done.1), custom_call_target="tpu_custom_call" | custom-call | tf_op jit(solution)/shard_map/pallas_call | solution.py:670
Async XLA Ops:
  63.0 1.2 %copy-start = (bf16[2048,256]{1,0:T(8,128)(2,1)S(1)}, bf16[2048,256]{1,0:T(8,128)(2,1)}, u32[]{:S(2)}) copy-start(bf16[2048,256]{1,0:T(8,128)(2,1)} %get-tuple-element.14.gnodes) | copy-start | bytes 3145732
  64.2 1.1 %copy-start.1 = (bf16[2,784,256]{2,1,0:T(8,128)(2,1)S(1)}, bf16[2,784,256]{2,1,0:T(8,128)(2,1)}, u32[]{:S(2)}) copy-start(bf16[2,784,256]{2,1,0:T(8,128)(2,1)} %get-tuple-element.15.gw) | copy-start | bytes 2408452
  65.3 0.7 %copy-start.2 = (bf16[32,256]{1,0:T(8,128)(2,1)S(1)}, bf16[32,256]{1,0:T(8,128)(2,1)}, u32[]{:S(2)}) copy-start(bf16[32,256]{1,0:T(8,128)(2,1)} %get-tuple-element.13.pooled) | copy-start | bytes 49156

commit v3 on v2

--- a/solution.py
+++ b/solution.py
@@ -424,9 +424,9 @@
                 pl.when(me == d)(bias_gathers[d - 1].wait_recv)
             bias_forward.start()
 
+    grads = dnt(xt[...], gp[...])
     for c in range(2):
-        first = dnt(xt[...], gp[c * HW : (c + 1) * HW, :])
-        pwf[c, 0:528, :] = first
+        pwf[c, 0:528, :] = grads[:, c * HW : (c + 1) * HW]
     to_pair(0)
 
     w2v = w2[...]
@@ -567,23 +567,52 @@
         copy.wait()
 
 
-def finish(scale, pooled, gnodes, gw, pooled_o, gnodes_o, first_o, bias_o, second_o, buf, sems):
-    moves = [
-        pltpu.make_async_copy(gw, buf, sems.at[0]),
-        pltpu.make_async_copy(gnodes, gnodes_o, sems.at[1]),
-        pltpu.make_async_copy(pooled, pooled_o, sems.at[2]),
-    ]
-    for copy in moves:
+def finish(
+    scale,
+    pooled,
+    gnodes,
+    gw,
+    pooled_o,
+    gnodes_o,
+    first_o,
+    bias_o,
+    second_o,
+    pooled_v,
+    gnodes_v,
+    gw_v,
+    first_v,
+    bias_v,
+    second_v,
+    sems,
+):
+    def move(source, target, number):
+        copy = pltpu.make_async_copy(source, target, sems.at[number])
         copy.start()
-    moves[0].wait()
+        return copy
+
+    coming = [move(gw.at[c], gw_v.at[c], c) for c in range(2)]
+    parts = [pl.ds(i * (N // 2), N // 2) for i in range(2)]
+    rows = [move(gnodes.at[part], gnodes_v.at[part], 2 + i) for i, part in enumerate(parts)]
+    small = move(pooled, pooled_v, 4)
     unit = eye(HW)
+    going = []
     for c in range(2):
         half = slice(c * HW, (c + 1) * HW)
-        first_o[:, half] = buf[c, 0:512, :].astype(F32) * scale
-        bias_o[:, half] = buf[c, 512:528, :].astype(F32)[:1] * scale
-        second_o[half, :] = dnt(unit, buf[c, 528:784, :]) * scale
-    moves[1].wait()
-    moves[2].wait()
+        coming[c].wait()
+        first_v[:, half] = gw_v[c, 0:512, :].astype(F32) * scale
+        bias_v[:, half] = gw_v[c, 512:528, :].astype(F32)[:1] * scale
+        second_v[half, :] = dnt(unit, gw_v[c, 528:784, :]) * scale
+        place = pl.ds(c * HW, HW)
+        going.append(move(second_v.at[place], second_o.at[place], 5 + c))
+    going.append(move(first_v, first_o, 7))
+    going.append(move(bias_v, bias_o, 8))
+    for i, part in enumerate(parts):
+        rows[i].wait()
+        going.append(move(gnodes_v.at[part], gnodes_o.at[part], 9 + i))
+    small.wait()
+    going.append(move(pooled_v, pooled_o, 11))
+    for copy in going:
+        copy.wait()
 
 
 def local(nodes, brows, src, tgt, mask, segs, w1, b1, w2, cot):
@@ -652,7 +681,6 @@
     ):
         scratch += [dma(shape), dma(shape)]
     anywhere = pl.BlockSpec(memory_space=pl.ANY)
-    vmem = pl.BlockSpec(memory_space=pltpu.VMEM)
     outs = (
         jax.ShapeDtypeStruct((SR, F), BF),
         jax.ShapeDtypeStruct((N, F), BF),
@@ -676,9 +704,17 @@
             jax.ShapeDtypeStruct((H, F), F32),
         ),
         in_specs=[anywhere] * 3,
-        out_specs=(anywhere, anywhere, vmem, vmem, vmem),
-        scratch_shapes=[pltpu.VMEM((2, PW, HW), BF), dma((3,))],
-        compiler_params=pltpu.CompilerParams(vmem_limit_bytes=16 * 2**20),
+        out_specs=(anywhere,) * 5,
+        scratch_shapes=[
+            pltpu.VMEM((SR, F), BF),
+            pltpu.VMEM((N, F), BF),
+            pltpu.VMEM((2, PW, HW), BF),
+            pltpu.VMEM((H, H), F32),
+            pltpu.VMEM((1, H), F32),
+            pltpu.VMEM((H, F), F32),
+            dma((12,)),
+        ],
+        compiler_params=pltpu.CompilerParams(vmem_limit_bytes=60 * 2**20),
     )(pooled, gnodes, gw)
     return pooled, gnodes, first, bias.reshape(H), second
 

time: 68.7 us -> 66.3 us (0.965)
  local copies, waits for them, and re-layouts: 3.07 us -> 0 us
  Pallas kernels: 64.5 us -> 65.4 us
    unnamed x6 -> x0, local copies, waits for them, and re-layouts: 3.07 us -> none
    pallas_call x1, Pallas kernels: 2.21 us -> 3.03 us  [local(): pl.pallas_call(functools.partial(finish, float((E * GX * GY) ** (-0.5))),...]
where the time goes in v3:
time: 66.3 us; the launch traced here: 66.2 us
  Pallas kernels  65.4 us (99%)
  between operations  0.8 us (1%)
    pallas_call x1, Pallas kernels, local(): pl.pallas_call(kernel, out_shape=(*outs, jax.ShapeDtypeStruct((2, PW, HW)...  62.3 us
    pallas_call x1, Pallas kernels, local(): pl.pallas_call(functools.partial(finish, float((E * GX * GY) ** (-0.5))),...  3.03 us

profile of v3, /device:TPU:1, one launch (start us, length us, event | category | flops | bytes accessed | tf_op | source)
XLA Modules:
  0.0 66.2 jit_solution(8738619607728262623)
XLA Ops:
  0.6 62.3 %shard_map.137 = (bf16[32,256]{1,0:T(8,128)(2,1)}, bf16[2048,256]{1,0:T(8,128)(2,1)}, bf16[2,784,256]{2,1,0:T(8,128)(2,1)}) custom-call(bf16[2048,256]{1,0:T(8,128)(2,1)} %nodes_h.1, s32[1,128]{1,0:T(1,128)} %bitcast.6, s32[32,128]{1,0:T(8,128)} %src_h.1, s32[32,128]{1,0:T(8,128)} %tgt_h.1, s32[32,128]{1,0:T(8,128)} %mask_h.1, s32[16,128]{1,0:T(8,128)} %bitcast.4, ...), custom_call_target="tpu_custom_call" | custom-call | tf_op jit(solution)/shard_map/pallas_call | solution.py:688
  63.0 3.0 %shard_map.138 = (bf16[32,256]{1,0:T(8,128)(2,1)}, bf16[2048,256]{1,0:T(8,128)(2,1)}, f32[512,512]{1,0:T(8,128)}, f32[1,512]{1,0:T(1,128)}, f32[512,256]{1,0:T(8,128)}) custom-call(bf16[32,256]{1,0:T(8,128)(2,1)} %get-tuple-element.13.pooled, bf16[2048,256]{1,0:T(8,128)(2,1)} %get-tuple-element.14.gnodes, bf16[2,784,256]{2,1,0:T(8,128)(2,1)} %get-tuple-element.15.gw), custom_call_target="tpu_custom_call" | custom-call | tf_op jit(solution)/shard_map/pallas_call | solution.py:698

commit v4 on v3

--- a/solution.py
+++ b/solution.py
@@ -21,6 +21,11 @@
 GX = 16
 GY = 8
 W = 1024
+T = 256
+TILES = (N + HALO) // T
+RUNS = E // T
+STEPS = TILES + RUNS - 1
+KINDS = 12
 PW = 784
 HW = H // 2
 NT = (((1,), (1,)), ((), ()))
@@ -47,6 +52,65 @@
     a = lax.broadcasted_iota(jnp.int32, (size, size), 0)
     b = lax.broadcasted_iota(jnp.int32, (size, size), 1)
     return jnp.where(a == b, 1.0, 0.0).astype(BF)
+
+
+def ordered(size, earlier_row):
+    a = lax.broadcasted_iota(jnp.int32, (size, size), 0)
+    b = lax.broadcasted_iota(jnp.int32, (size, size), 1)
+    return jnp.where(a < b if earlier_row else b < a, 1.0, 0.0).astype(BF)
+
+
+def sort_edges(src, tgt, mask, spot, plan):
+    tile = jnp.right_shift(src[...], 8)
+    inside = jnp.concatenate(
+        [jnp.where(tile == j, 1.0, 0.0).astype(BF) for j in range(KINDS)], axis=0
+    )
+    before = dot(inside, ordered(128, True))
+    counts = dot(inside, jnp.ones((128, 128), BF)).astype(BF)
+    base = dot(ordered(32 * KINDS, False), counts)
+    places = jnp.zeros((32, 128), F32)
+    for j in range(TILES):
+        rows = slice(32 * j, 32 * j + 32)
+        places = places + jnp.where(tile == j, before[rows] + base[rows], 0.0)
+    spot[...] = places.astype(jnp.int32)
+
+    place = id_row(spot, 0, 32)
+    sources = id_row(src, 0, 32)
+    targets = id_row(tgt, 0, 32)
+    live = id_row(mask, 0, 32)
+    here = lax.broadcasted_iota(jnp.int32, (32, E), 0) == jnp.right_shift(place, 7)
+    parts = (
+        jnp.bitwise_and(sources, 255),
+        jnp.bitwise_and(targets, 255),
+        jnp.right_shift(sources, 8) * 16 + jnp.right_shift(targets, 8),
+        live,
+    )
+    parts = [jnp.where(here, part.astype(F32), 0.0).astype(BF) for part in parts]
+    moved = dnt(
+        jnp.concatenate(parts, axis=0), one_hot(jnp.bitwise_and(place, 127), 0, 128)
+    ).astype(jnp.int32)
+    upper = moved[64:96]
+    src[...] = moved[0:32] + 256 * jnp.right_shift(upper, 4)
+    tgt[...] = moved[32:64] + 256 * jnp.bitwise_and(upper, 15)
+    mask[...] = moved[96:128]
+
+    lane = lax.broadcasted_iota(jnp.int32, (1, 128), 1)
+    border = jnp.zeros((1, 128), F32)
+    for j in range(1, TILES):
+        border = jnp.where(lane == j, base[32 * j : 32 * j + 1], border)
+    passed = jnp.minimum(jnp.right_shift(border.astype(jnp.int32), 8), RUNS - 1)
+    rank = jnp.where((lane >= 1) & (lane < TILES), lane - 1 + passed, 1000)
+    step = lax.broadcasted_iota(jnp.int32, (32, 128), 0)
+    wide = lax.broadcasted_iota(jnp.int32, (32, 128), 1)
+    table_tile = jnp.sum(jnp.where(rank < step, 1.0, 0.0), axis=1, keepdims=True).astype(
+        jnp.int32
+    )
+    table_tile = jnp.broadcast_to(table_tile, (32, 128))
+    edge_tile = step - table_tile
+    plan[0:32, :] = jnp.where(wide == 0, edge_tile, table_tile)
+    for row, which in ((32, edge_tile), (33, table_tile)):
+        upto = jnp.where((which <= wide) & (step < STEPS), 1.0, 0.0)
+        plan[row : row + 1, :] = jnp.sum(upto, axis=0, keepdims=True).astype(jnp.int32) - 1
 
 
 def split(value):
@@ -81,6 +145,14 @@
     pooled,
     gnodes,
     tt,
+    tiles,
+    spot,
+    plan_v,
+    plan,
+    xs,
+    gis,
+    sums_s,
+    run,
     w1t,
     bcol,
     bnd,
@@ -110,6 +182,7 @@
     acc,
     in_s,
     out_s,
+    plan_s,
     h_s,
     h_r,
     c_s,
@@ -180,8 +253,8 @@
     unit = eye(F)
     for copy in loads[:3]:
         copy.wait()
-    tt[:, :N] = dnt(unit, nodes[...]).astype(BF)
-    bnd[...] = dot(tt[:, :N], one_hot(brows[...], 0, N)).astype(BF)
+    tt[...] = dnt(unit, nodes[...]).astype(BF)
+    bnd[...] = dot(tt[...], one_hot(brows[...], 0, N)).astype(BF)
     line[pl.ds(me, 1)] = cot[...][None]
 
     pl.semaphore_wait(barrier, GX - 1 + GY - 1)
@@ -210,6 +283,12 @@
     for copy in loads[3:]:
         copy.wait()
 
+    sort_edges(src, tgt, mask, spot, plan_v)
+    to_plan = pltpu.make_async_copy(plan_v, plan, plan_s)
+    to_plan.start()
+    for j in range(N // T):
+        tiles[j] = tt[:, j * T : (j + 1) * T]
+
     for i in range(2):
         for j in range(2):
             w1t[j * F : (j + 1) * F, i * F : (i + 1) * F] = dnt(
@@ -233,7 +312,6 @@
 
     def gather(b, carry):
         targets = id_row(tgt, b * 8, 8)
-        sources = id_row(src, b * 8, 8)
         live = id_row(mask, b * 8, 8)
         low = one_hot(jnp.bitwise_and(targets, 127), 0, 128)
         found = dot(seg_parts, low)
@@ -242,8 +320,7 @@
         segment = jnp.sum(jnp.where(high, found, 0.0), axis=0, keepdims=True)
         segment = jnp.where(live > 0, segment, -1.0).astype(jnp.int32)
         mseg[:, block(b)] = jnp.broadcast_to(segment, (8, W))
-        xt[F : 2 * F, block(b)] = dot(tt[:, :N], one_hot(targets, 0, N)).astype(BF)
-        xt[:F, block(b)] = dot(tt[:, :N], one_hot(sources, 0, N)).astype(BF)
+        xt[F : 2 * F, block(b)] = dot(tt[...], one_hot(targets, 0, N)).astype(BF)
         return carry
 
     lax.fori_loop(0, E // W, gather, 0)
@@ -255,17 +332,41 @@
         def _(k=k):
             hrecv[k] = jnp.zeros((F, NB), BF)
 
-        tt[:, N + k * NB : N + (k + 1) * NB] = hrecv[k]
+    for j in range(2):
+        tiles[N // T + j] = jnp.concatenate([hrecv[2 * j], hrecv[2 * j + 1]], axis=1)
     for copy in cots:
         copy.wait_recv()
     lines = jnp.concatenate([line[g] for g in range(GX)], axis=0)
     line_t[...] = dnt(unit, lines).astype(BF)
 
+    to_plan.wait()
+
+    def planned(row, column, count):
+        return jnp.clip(plan[row, column], 0, count - 1)
+
+    def meeting(p):
+        run_of, tile_of = planned(p, 0, RUNS), planned(p, 1, TILES)
+        earlier = jnp.maximum(p - 1, 0)
+        hot = one_hot(id_row(src, run_of * (T // 128), T // 128), tile_of * T, T)
+        return run_of, tile_of, earlier, hot
+
+    def source_rows(g, carry):
+        total = run[...]
+        for k in range(5):
+            p = g * 5 + k
+            run_of, tile_of, earlier, hot = meeting(p)
+            same = planned(earlier, 0, RUNS) == run_of
+            total = jnp.where(same, total, 0.0) + dot(tiles[tile_of], hot)
+            xs[p] = total.astype(BF)
+        run[...] = total
+        return carry
+
+    run[...] = jnp.zeros_like(run)
+    lax.fori_loop(0, STEPS // 5, source_rows, 0)
+
     def edges(b, carry):
-        sources = id_row(src, b * 8, 8)
-        xt[:F, block(b)] = (
-            xt[:F, block(b)].astype(F32) + dot(tt[:, N:], one_hot(sources, N, HALO))
-        ).astype(BF)
+        for k in range(W // T):
+            xt[:F, block(b * (W // T) + k, T)] = xs[planned(32, b * (W // T) + k, STEPS)]
         chosen = one_hot(mseg[:1, block(b)], 0, SEG)
         gm = dot(line_t[...], chosen).astype(BF)
         bias = jnp.concatenate([bcol[...]] * (W // 128), axis=1)
@@ -463,17 +564,34 @@
         copy.start()
 
     def input_grads(b, carry):
-        gi[:, block(b)] = dot(w1[...], gp[:, block(b)]).astype(BF)
+        grads = dot(w1[...], gp[:, block(b)]).astype(BF)
+        gi[:, block(b)] = grads[F:]
+        for k in range(W // T):
+            gis[b * (W // T) + k] = grads[:F, k * T : (k + 1) * T]
         return carry
 
     lax.fori_loop(0, E // W, input_grads, 0)
     to_members(1)
     to_z(0)
 
-    all_src = id_row(src, 0, 32)
-    slots = dnt(one_hot(all_src, N, HALO), gi[:F, :])
-    for k in range(4):
-        gslot[k] = slots[k * NB : (k + 1) * NB].astype(BF)
+    def source_sums(g, carry):
+        total = run[...]
+        for k in range(5):
+            p = g * 5 + k
+            run_of, tile_of, earlier, hot = meeting(p)
+            same = planned(earlier, 1, TILES) == tile_of
+            total = jnp.where(same, total, 0.0) + dnt(hot, gis[run_of])
+            sums_s[p] = total
+        run[...] = total
+        return carry
+
+    run[...] = jnp.zeros_like(run)
+    lax.fori_loop(0, STEPS // 5, source_sums, 0)
+
+    for j in range(2):
+        slots = sums_s[planned(33, N // T + j, STEPS)].astype(BF)
+        gslot[2 * j] = slots[:NB]
+        gslot[2 * j + 1] = slots[NB:]
     back = (
         remote(gslot.at[0], gret.at[0], g_s.at[0], g_r.at[0], {"gx": lax.rem(me + GX - 1, GX)}),
         remote(gslot.at[1], gret.at[1], g_s.at[1], g_r.at[1], {"gx": lax.rem(me + 1, GX)}),
@@ -485,8 +603,10 @@
 
     def own(b, carry):
         first = b * 512
-        s = dnt(one_hot(id_row(src, 0, 32), first, 512), gi[:F, :])
-        t = dnt(one_hot(id_row(tgt, 0, 32), first, 512), gi[F:, :])
+        s = jnp.concatenate(
+            [sums_s[planned(33, b * 2 + k, STEPS)] for k in range(2)], axis=0
+        )
+        t = dnt(one_hot(id_row(tgt, 0, 32), first, 512), gi[...])
         acc[block(b, 512), :] = s + t
 
         @pl.when(b == 0)
@@ -495,8 +615,7 @@
             to_all(0)
 
         pl.when(b == 1)(functools.partial(to_all, 1))
-        pl.when(b == 2)(functools.partial(to_other_core, 0))
-        pl.when(b == 3)(functools.partial(to_other_core, 1))
+        pl.when(b == 3)(functools.partial(to_other_core, 0))
         return carry
 
     lax.fori_loop(0, N // 512, own, 0)
@@ -540,6 +659,7 @@
     stores.append(pltpu.make_async_copy(pooled, pooled_h, out_s.at[4]))
     stores[-1].start()
 
+    to_other_core(1)
     for part in range(2):
         for copy in forwards[part]:
             copy.wait_recv()
@@ -634,7 +754,15 @@
     scratch += [
         pltpu.VMEM((SR, F), BF),
         pltpu.VMEM((N, F), BF),
-        pltpu.VMEM((F, N + HALO), BF),
+        pltpu.VMEM((F, N), BF),
+        pltpu.VMEM((TILES, F, T), BF),
+        pltpu.VMEM((32, 128), int32),
+        pltpu.VMEM((40, 128), int32),
+        pltpu.SMEM((40, 128), int32),
+        pltpu.VMEM((STEPS, F, T), BF),
+        pltpu.VMEM((RUNS, F, T), BF),
+        pltpu.VMEM((STEPS, T, F), F32),
+        pltpu.VMEM((T, F), F32),
         pltpu.VMEM((H, 2 * F), BF),
         pltpu.VMEM((H, 128), F32),
         pltpu.VMEM((F, NB), BF),
@@ -645,7 +773,7 @@
         pltpu.VMEM((8, E), int32),
         pltpu.VMEM((H, E), BF),
         pltpu.VMEM((H, E), BF),
-        pltpu.VMEM((2 * F, E), BF),
+        pltpu.VMEM((F, E), BF),
         pltpu.VMEM((2, PW, HW), F32),
         pltpu.VMEM((2, PW, HW), BF),
         pltpu.VMEM((PW, HW), BF),
@@ -664,6 +792,7 @@
         pltpu.VMEM((N, F), F32),
         dma((10,)),
         dma((6,)),
+        dma,
     ]
     for shape in (
         (4,),

time: 66.3 us -> 64.1 us (0.967)
  Pallas kernels: 65.4 us -> 63.2 us
    pallas_call x1, Pallas kernels: 62.3 us -> 60.1 us  [local(): pl.pallas_call(kernel, out_shape=(*outs, jax.ShapeDtypeStruct((2, PW, HW)...]
where the time goes in v4:
time: 64.1 us; the launch traced here: 64 us
  Pallas kernels  63.2 us (99%)
  between operations  0.8 us (1%)
    pallas_call x1, Pallas kernels, local(): pl.pallas_call(kernel, out_shape=(*outs, jax.ShapeDtypeStruct((2, PW, HW)...  60.1 us
    pallas_call x1, Pallas kernels, local(): pl.pallas_call(functools.partial(finish, float((E * GX * GY) ** (-0.5))),...  3.04 us

profile of v4, /device:TPU:1, one launch (start us, length us, event | category | flops | bytes accessed | tf_op | source)
XLA Modules:
  0.0 64.0 jit_solution(758468768604114301)
XLA Ops:
  0.6 60.1 %shard_map.137 = (bf16[32,256]{1,0:T(8,128)(2,1)}, bf16[2048,256]{1,0:T(8,128)(2,1)}, bf16[2,784,256]{2,1,0:T(8,128)(2,1)}) custom-call(bf16[2048,256]{1,0:T(8,128)(2,1)} %nodes_h.1, s32[1,128]{1,0:T(1,128)} %bitcast.6, s32[32,128]{1,0:T(8,128)} %src_h.1, s32[32,128]{1,0:T(8,128)} %tgt_h.1, s32[32,128]{1,0:T(8,128)} %mask_h.1, s32[16,128]{1,0:T(8,128)} %bitcast.4, ...), custom_call_target="tpu_custom_call" | custom-call | tf_op jit(solution)/shard_map/pallas_call | solution.py:817
  60.8 3.0 %shard_map.138 = (bf16[32,256]{1,0:T(8,128)(2,1)}, bf16[2048,256]{1,0:T(8,128)(2,1)}, f32[512,512]{1,0:T(8,128)}, f32[1,512]{1,0:T(1,128)}, f32[512,256]{1,0:T(8,128)}) custom-call(bf16[32,256]{1,0:T(8,128)(2,1)} %get-tuple-element.13.pooled, bf16[2048,256]{1,0:T(8,128)(2,1)} %get-tuple-element.14.gnodes, bf16[2,784,256]{2,1,0:T(8,128)(2,1)} %get-tuple-element.15.gw), custom_call_target="tpu_custom_call" | custom-call | tf_op jit(solution)/shard_map/pallas_call | solution.py:827

commit v5 on v4

--- a/solution.py
+++ b/solution.py
@@ -175,6 +175,7 @@
     zb_b,
     zbias,
     ag,
+    psum,
     psend,
     precv,
     gslot,
@@ -539,7 +540,8 @@
         node_hot = one_hot(id_row(segs, 0, N // 128), first, 256)
         part = dot(high, w2v) + dot(low, w2v) + dot(node_hot, nodes[...])
         for i in range(8):
-            psend[b * 8 + i] = part[i * SR : (i + 1) * SR]
+            psum[b * 8 + i] = part[i * SR : (i + 1) * SR]
+            psend[b * 8 + i] = part[i * SR : (i + 1) * SR].astype(BF)
         lines_t = line_t[:, block(b, 256)]
         add = dot(lines_t, high) + dot(lines_t, low)
         for c in range(2):
@@ -560,9 +562,6 @@
         )
         for d in range(1, GX)
     ]
-    for copy in pools:
-        copy.start()
-
     def input_grads(b, carry):
         grads = dot(w1[...], gp[:, block(b)]).astype(BF)
         gi[:, block(b)] = grads[F:]
@@ -573,6 +572,8 @@
     lax.fori_loop(0, E // W, input_grads, 0)
     to_members(1)
     to_z(0)
+    for copy in pools:
+        copy.start()
 
     def source_sums(g, carry):
         total = run[...]
@@ -615,7 +616,6 @@
             to_all(0)
 
         pl.when(b == 1)(functools.partial(to_all, 1))
-        pl.when(b == 3)(functools.partial(to_other_core, 0))
         return carry
 
     lax.fori_loop(0, N // 512, own, 0)
@@ -650,11 +650,13 @@
             )
             stores[-1].start()
 
+    to_other_core(0)
+
     for copy in pools:
         copy.wait_recv()
-    sums = psend[me]
+    sums = psum[me]
     for d in range(1, GX):
-        sums = sums + precv[d]
+        sums = sums + precv[d].astype(F32)
     pooled[...] = sums.astype(BF)
     stores.append(pltpu.make_async_copy(pooled, pooled_h, out_s.at[4]))
     stores[-1].start()
@@ -786,7 +788,8 @@
         pltpu.VMEM((4, 16, HW), F32),
         pltpu.VMEM((2, PW, HW), BF),
         pltpu.VMEM((GX, SR, F), F32),
-        pltpu.VMEM((GX, SR, F), F32),
+        pltpu.VMEM((GX, SR, F), BF),
+        pltpu.VMEM((GX, SR, F), BF),
         pltpu.VMEM((4, NB, F), BF),
         pltpu.VMEM((4, NB, F), BF),
         pltpu.VMEM((N, F), F32),

time: 64.1 us -> 60.3 us (0.941)
  Pallas kernels: 63.2 us -> 59.3 us
    pallas_call x1, Pallas kernels: 60.1 us -> 56.3 us  [local(): pl.pallas_call(kernel, out_shape=(*outs, jax.ShapeDtypeStruct((2, PW, HW)...]
where the time goes in v5:
time: 60.3 us; the launch traced here: 60.1 us
  Pallas kernels  59.3 us (98%)
  between operations  0.8 us (1%)
    pallas_call x1, Pallas kernels, local(): pl.pallas_call(kernel, out_shape=(*outs, jax.ShapeDtypeStruct((2, PW, HW)...  56.3 us
    pallas_call x1, Pallas kernels, local(): pl.pallas_call(functools.partial(finish, float((E * GX * GY) ** (-0.5))),...  3.04 us

profile of v5, /device:TPU:1, one launch (start us, length us, event | category | flops | bytes accessed | tf_op | source)
XLA Modules:
  0.0 60.1 jit_solution(5079675282753423863)
XLA Ops:
  0.6 56.3 %shard_map.137 = (bf16[32,256]{1,0:T(8,128)(2,1)}, bf16[2048,256]{1,0:T(8,128)(2,1)}, bf16[2,784,256]{2,1,0:T(8,128)(2,1)}) custom-call(bf16[2048,256]{1,0:T(8,128)(2,1)} %nodes_h.1, s32[1,128]{1,0:T(1,128)} %bitcast.6, s32[32,128]{1,0:T(8,128)} %src_h.1, s32[32,128]{1,0:T(8,128)} %tgt_h.1, s32[32,128]{1,0:T(8,128)} %mask_h.1, s32[16,128]{1,0:T(8,128)} %bitcast.4, ...), custom_call_target="tpu_custom_call" | custom-call | tf_op jit(solution)/shard_map/pallas_call | solution.py:820
  56.9 3.0 %shard_map.138 = (bf16[32,256]{1,0:T(8,128)(2,1)}, bf16[2048,256]{1,0:T(8,128)(2,1)}, f32[512,512]{1,0:T(8,128)}, f32[1,512]{1,0:T(1,128)}, f32[512,256]{1,0:T(8,128)}) custom-call(bf16[32,256]{1,0:T(8,128)(2,1)} %get-tuple-element.13.pooled, bf16[2048,256]{1,0:T(8,128)(2,1)} %get-tuple-element.14.gnodes, bf16[2,784,256]{2,1,0:T(8,128)(2,1)} %get-tuple-element.15.gw), custom_call_target="tpu_custom_call" | custom-call | tf_op jit(solution)/shard_map/pallas_call | solution.py:830

commit v6 on v5

--- a/solution.py
+++ b/solution.py
@@ -236,23 +236,29 @@
         )
 
     pairs = (
+        (src_h, src),
+        (tgt_h, tgt),
+        (mask_h, mask),
         (nodes_h, nodes),
         (brows_h, brows),
         (cot_h, cot),
+        (segs_h, segs),
         (w1_h, w1),
         (b1_h, b1),
-        (segs_h, segs),
-        (tgt_h, tgt),
-        (src_h, src),
-        (mask_h, mask),
         (w2_h, w2),
     )
     loads = [pltpu.make_async_copy(a, b, in_s.at[i]) for i, (a, b) in enumerate(pairs)]
     for copy in loads:
         copy.start()
 
+    for copy in loads[:3]:
+        copy.wait()
+    sort_edges(src, tgt, mask, spot, plan_v)
+    to_plan = pltpu.make_async_copy(plan_v, plan, plan_s)
+    to_plan.start()
+
     unit = eye(F)
-    for copy in loads[:3]:
+    for copy in loads[3:6]:
         copy.wait()
     tt[...] = dnt(unit, nodes[...]).astype(BF)
     bnd[...] = dot(tt[...], one_hot(brows[...], 0, N)).astype(BF)
@@ -273,20 +279,17 @@
         remote(
             cot,
             line.at[me],
-            c_s.at[d],
-            c_r.at[d],
+            c_s,
+            c_r,
             {"gx": lax.rem(me + d, GX)},
         )
         for d in range(1, GX)
     ]
     for copy in cots:
         copy.start()
-    for copy in loads[3:]:
+    for copy in loads[6:]:
         copy.wait()
 
-    sort_edges(src, tgt, mask, spot, plan_v)
-    to_plan = pltpu.make_async_copy(plan_v, plan, plan_s)
-    to_plan.start()
     for j in range(N // T):
         tiles[j] = tt[:, j * T : (j + 1) * T]
 
@@ -335,8 +338,9 @@
 
     for j in range(2):
         tiles[N // T + j] = jnp.concatenate([hrecv[2 * j], hrecv[2 * j + 1]], axis=1)
-    for copy in cots:
-        copy.wait_recv()
+    others = line.at[pl.ds(1, GX - 1)]
+    all_cots = remote(others, others, c_s, c_r, {"gx": me})
+    all_cots.wait_recv()
     lines = jnp.concatenate([line[g] for g in range(GX)], axis=0)
     line_t[...] = dnt(unit, lines).astype(BF)
 
@@ -374,12 +378,11 @@
         x = dot(w1t[...], xt[: 2 * F, block(b)]) + bias
         gh = dot(w2[...], gm)
         square = x * x
-        t = jnp.tanh(x * (0.7978845608028654 + 0.035677408136300125 * square))
-        half = 0.5 + 0.5 * t
-        hid[:, block(b)] = (x * half).astype(BF)
-        slope = half + (0.5 * x) * (1.0 - t * t) * (
-            0.7978845608028654 + 0.10703222440890037 * square
-        )
+        t = 0.5 * jnp.tanh(x * (0.7978845608028654 + 0.035677408136300125 * square))
+        half = 0.5 + t
+        h = x * half
+        hid[:, block(b)] = h.astype(BF)
+        slope = half + (h * (0.5 - t)) * (1.5957691216057308 + 0.21406444881780074 * square)
         gp[:, block(b)] = (gh * slope).astype(BF)
         return carry
 
@@ -398,6 +401,7 @@
 
     peers = [lax.rem(me + d, GX) for d in range(GX)]
     pair, scatter, over_z, gathers, forwards = [], [], [], [], []
+    all_scatter, all_z, all_gathers = [], [], []
     for part in range(2):
         pair.append(
             remote(
@@ -413,8 +417,8 @@
                 remote(
                     csum.at[rows_of(part, peers[d])],
                     arrived[part].at[d],
-                    rs_s.at[part, d],
-                    rs_r.at[part, d],
+                    rs_s.at[part],
+                    rs_r.at[part],
                     {"gx": peers[d]},
                 )
                 for d in range(1, GX)
@@ -425,8 +429,8 @@
                 remote(
                     by_z[part].at[z],
                     by_z[part].at[z],
-                    z_s.at[part, d],
-                    z_r.at[part, d],
+                    z_s.at[part],
+                    z_r.at[part],
                     {"gy": lax.rem(my + 2 * d, GY)},
                 )
                 for d in range(1, 4)
@@ -435,30 +439,38 @@
         place = ag.at[core, rows_of(part, me)]
         gathers.append(
             [
-                remote(place, place, ag_s.at[part, d], ag_r.at[part, d], {"gx": peers[d]})
+                remote(place, place, ag_s.at[part], ag_r.at[part], {"gx": peers[d]})
                 for d in range(1, GX)
             ]
         )
-        ways = []
-        for d in range(GX):
-            place = ag.at[core, rows_of(part, lax.rem(me + GX - d, GX))]
-            ways.append(remote(place, place, fw_s.at[part, d], fw_r.at[part, d], {"gy": sib}))
-        forwards.append(ways)
+        place = ag.at[core, whole(part)]
+        forwards.append(remote(place, place, fw_s.at[part], fw_r.at[part], {"gy": sib}))
+        others = arrived[part].at[pl.ds(1, GX - 1)]
+        all_scatter.append(remote(others, others, rs_s.at[part], rs_r.at[part], {"gx": me}))
+        others = by_z[part].at[pl.ds(0, 3)]
+        all_z.append(remote(others, others, z_s.at[part], z_r.at[part], {"gy": my}))
+        others = ag.at[core, pl.ds(firsts[part], (GX - 1) * shares[part])]
+        all_gathers.append(remote(others, others, ag_s.at[part], ag_r.at[part], {"gx": me}))
     bias_rows = csum.at[pl.ds(512, 16)]
     bias_scatter = [
-        remote(bias_rows, rsbias.at[d], rb_s.at[d], rb_r.at[d], {"gx": peers[d]})
+        remote(bias_rows, rsbias.at[d], rb_s, rb_r, {"gx": peers[d]})
         for d in range(1, GX)
     ]
     bias_z = [
-        remote(zbias.at[z], zbias.at[z], zb_s.at[d], zb_r.at[d], {"gy": lax.rem(my + 2 * d, GY)})
+        remote(zbias.at[z], zbias.at[z], zb_s, zb_r, {"gy": lax.rem(my + 2 * d, GY)})
         for d in range(1, 4)
     ]
     bias_place = ag.at[core, pl.ds(512, 16)]
     bias_gathers = [
-        remote(bias_place, bias_place, agb_s.at[d], agb_r.at[d], {"gx": peers[d]})
+        remote(bias_place, bias_place, agb_s, agb_r, {"gx": peers[d]})
         for d in range(1, GX)
     ]
-    bias_forward = remote(bias_place, bias_place, fw_s.at[0, GX], fw_r.at[0, GX], {"gy": sib})
+    others = rsbias.at[pl.ds(1, GX - 1)]
+    all_bias_scatter = remote(others, others, rb_s, rb_r, {"gx": me})
+    others = zbias.at[pl.ds(0, 3)]
+    all_bias_z = remote(others, others, zb_s, zb_r, {"gy": my})
+    others = ag.at[core, pl.ds(0, (GX - 1) * 16)]
+    all_bias_gathers = remote(others, others, agb_s, agb_r, {"gx": me})
 
     def to_pair(part):
         pws[:, whole(part), :] = pwf[:, whole(part), :].astype(BF)
@@ -476,8 +488,7 @@
                 pl.when(me + d == GX)(bias_scatter[d - 1].start)
 
     def to_z(part):
-        for copy in scatter[part]:
-            copy.wait_recv()
+        all_scatter[part].wait_recv()
         total = csum[rows_of(part, me), :].astype(F32)
         for d in range(1, GX):
             total = total + arrived[part][d].astype(F32)
@@ -488,8 +499,7 @@
 
             @pl.when(me == 0)
             def _():
-                for copy in bias_scatter:
-                    copy.wait_recv()
+                all_bias_scatter.wait_recv()
                 sums = csum[512:528, :].astype(F32)
                 for d in range(1, GX):
                     sums = sums + rsbias[d].astype(F32)
@@ -498,33 +508,27 @@
                     copy.start()
 
     def to_all(part):
-        for copy in over_z[part]:
-            copy.wait_recv()
+        all_z[part].wait_recv()
         sums = by_z[part]
         total = (sums[0] + sums[1]) + (sums[2] + sums[3])
         ag[pl.ds(core, 1), rows_of(part, me), :] = total.astype(BF)[None]
         for copy in gathers[part]:
             copy.start()
-        forwards[part][0].start()
         if part == 0:
 
             @pl.when(me == 0)
             def _():
-                for copy in bias_z:
-                    copy.wait_recv()
+                all_bias_z.wait_recv()
                 sums = (zbias[0] + zbias[1]) + (zbias[2] + zbias[3])
                 ag[pl.ds(core, 1), 512:528, :] = sums.astype(BF)[None]
                 for copy in bias_gathers:
                     copy.start()
 
     def to_other_core(part):
-        for d in range(1, GX):
-            gathers[part][d - 1].wait_recv()
-            forwards[part][d].start()
+        all_gathers[part].wait_recv()
         if part == 0:
-            for d in range(1, GX):
-                pl.when(me == d)(bias_gathers[d - 1].wait_recv)
-            bias_forward.start()
+            pl.when(me > 0)(bias_gathers[0].wait_recv)
+        forwards[part].start()
 
     grads = dnt(xt[...], gp[...])
     for c in range(2):
@@ -556,8 +560,8 @@
         remote(
             psend.at[peers[d]],
             precv.at[d],
-            p_s.at[d],
-            p_r.at[d],
+            p_s,
+            p_r,
             {"gx": peers[d]},
         )
         for d in range(1, GX)
@@ -652,8 +656,9 @@
 
     to_other_core(0)
 
-    for copy in pools:
-        copy.wait_recv()
+    others = precv.at[pl.ds(1, GX - 1)]
+    all_pools = remote(others, others, p_s, p_r, {"gx": me})
+    all_pools.wait_recv()
     sums = psum[me]
     for d in range(1, GX):
         sums = sums + precv[d].astype(F32)
@@ -662,28 +667,23 @@
     stores[-1].start()
 
     to_other_core(1)
-    for part in range(2):
-        for copy in forwards[part]:
-            copy.wait_recv()
-    bias_forward.wait_recv()
+    for copy in forwards:
+        copy.wait_recv()
     stores.append(pltpu.make_async_copy(ag, gw_h, out_s.at[5]))
     stores[-1].start()
 
     for k in range(4):
         pl.when(there[k])(halo[k].wait_send)
         pl.when(there[k])(back[k].wait_send)
-    for group in (cots, pools, pair, [bias_forward], *scatter, *over_z, *gathers, *forwards):
+    for group in ([all_cots, all_pools], pair, all_scatter, all_z, all_gathers, forwards):
         for copy in group:
             copy.wait_send()
-    for d in range(1, GX):
-        pl.when(me + d == GX)(bias_scatter[d - 1].wait_send)
+    pl.when(me > 0)(bias_scatter[0].wait_send)
 
     @pl.when(me == 0)
     def _():
-        for copy in bias_z:
-            copy.wait_send()
-        for copy in bias_gathers:
-            copy.wait_send()
+        all_bias_z.wait_send()
+        all_bias_gathers.wait_send()
 
     for copy in stores:
         copy.wait()
@@ -797,21 +797,32 @@
         dma((6,)),
         dma,
     ]
-    for shape in (
-        (4,),
-        (GX,),
-        (GX,),
-        (4,),
-        (2,),
-        (2, GX),
-        (GX,),
-        (2, 4),
-        (4,),
-        (2, GX),
-        (GX,),
-        (2, GX + 1),
-    ):
-        scratch += [dma(shape), dma(shape)]
+    scratch += [
+        dma((4,)),
+        dma((4,)),
+        dma,
+        dma,
+        dma,
+        dma,
+        dma((4,)),
+        dma((4,)),
+        dma((2,)),
+        dma((2,)),
+        dma((2,)),
+        dma((2,)),
+        dma,
+        dma,
+        dma((2,)),
+        dma((2,)),
+        dma,
+        dma,
+        dma((2,)),
+        dma((2,)),
+        dma,
+        dma,
+        dma((2,)),
+        dma((2,)),
+    ]
     anywhere = pl.BlockSpec(memory_space=pl.ANY)
     outs = (
         jax.ShapeDtypeStruct((SR, F), BF),

time: 60.3 us -> 57.6 us (0.955)
  Pallas kernels: 59.3 us -> 56.6 us
    pallas_call x1, Pallas kernels: 56.3 us -> 53.6 us  [local(): pl.pallas_call(kernel, out_shape=(*outs, jax.ShapeDtypeStruct((2, PW, HW)...]
where the time goes in v6:
time: 57.6 us; the launch traced here: 57.4 us
  Pallas kernels  56.6 us (98%)
  between operations  0.8 us (1%)
    pallas_call x1, Pallas kernels, local(): pl.pallas_call(kernel, out_shape=(*outs, jax.ShapeDtypeStruct((2, PW, HW)...  53.6 us
    pallas_call x1, Pallas kernels, local(): pl.pallas_call(functools.partial(finish, float((E * GX * GY) ** (-0.5))),...  3.03 us

profile of v6, /device:TPU:1, one launch (start us, length us, event | category | flops | bytes accessed | tf_op | source)
XLA Modules:
  0.0 57.4 jit_solution(1153901463565377015)
XLA Ops:
  0.6 53.6 %shard_map.137 = (bf16[32,256]{1,0:T(8,128)(2,1)}, bf16[2048,256]{1,0:T(8,128)(2,1)}, bf16[2,784,256]{2,1,0:T(8,128)(2,1)}) custom-call(bf16[2048,256]{1,0:T(8,128)(2,1)} %nodes_h.1, s32[1,128]{1,0:T(1,128)} %bitcast.6, s32[32,128]{1,0:T(8,128)} %src_h.1, s32[32,128]{1,0:T(8,128)} %tgt_h.1, s32[32,128]{1,0:T(8,128)} %mask_h.1, s32[16,128]{1,0:T(8,128)} %bitcast.4, ...), custom_call_target="tpu_custom_call" | custom-call | tf_op jit(solution)/shard_map/pallas_call | solution.py:831
  54.2 3.0 %shard_map.138 = (bf16[32,256]{1,0:T(8,128)(2,1)}, bf16[2048,256]{1,0:T(8,128)(2,1)}, f32[512,512]{1,0:T(8,128)}, f32[1,512]{1,0:T(1,128)}, f32[512,256]{1,0:T(8,128)}) custom-call(bf16[32,256]{1,0:T(8,128)(2,1)} %get-tuple-element.13.pooled, bf16[2048,256]{1,0:T(8,128)(2,1)} %get-tuple-element.14.gnodes, bf16[2,784,256]{2,1,0:T(8,128)(2,1)} %get-tuple-element.15.gw), custom_call_target="tpu_custom_call" | custom-call | tf_op jit(solution)/shard_map/pallas_call | solution.py:841

commit v7 on v6

--- a/solution.py
+++ b/solution.py
@@ -20,7 +20,7 @@
 SR = 32
 GX = 16
 GY = 8
-W = 1024
+W = 2048
 T = 256
 TILES = (N + HALO) // T
 RUNS = E // T
@@ -315,8 +315,8 @@
         return pl.ds(pl.multiple_of(b * width, width), width)
 
     def gather(b, carry):
-        targets = id_row(tgt, b * 8, 8)
-        live = id_row(mask, b * 8, 8)
+        targets = id_row(tgt, b * 16, 16)
+        live = id_row(mask, b * 16, 16)
         low = one_hot(jnp.bitwise_and(targets, 127), 0, 128)
         found = dot(seg_parts, low)
         found = found[:16] + 256.0 * found[16:]
@@ -726,8 +726,8 @@
         second_v[half, :] = dnt(unit, gw_v[c, 528:784, :]) * scale
         place = pl.ds(c * HW, HW)
         going.append(move(second_v.at[place], second_o.at[place], 5 + c))
-    going.append(move(first_v, first_o, 7))
-    going.append(move(bias_v, bias_o, 8))
+        going.append(move(first_v.at[:, place], first_o.at[:, place], 7 + c))
+    going.append(move(bias_v, bias_o, 12))
     for i, part in enumerate(parts):
         rows[i].wait()
         going.append(move(gnodes_v.at[part], gnodes_o.at[part], 9 + i))
@@ -855,7 +855,7 @@
             pltpu.VMEM((H, H), F32),
             pltpu.VMEM((1, H), F32),
             pltpu.VMEM((H, F), F32),
-            dma((12,)),
+            dma((13,)),
         ],
         compiler_params=pltpu.CompilerParams(vmem_limit_bytes=60 * 2**20),
     )(pooled, gnodes, gw)

time: 57.6 us -> 56.9 us (0.988)
  Pallas kernels: 56.6 us -> 56 us
where the time goes in v7:
time: 56.9 us; the launch traced here: 56.8 us
  Pallas kernels  56 us (98%)
  between operations  0.8 us (1%)
    pallas_call x1, Pallas kernels, local(): pl.pallas_call(kernel, out_shape=(*outs, jax.ShapeDtypeStruct((2, PW, HW)...  53.1 us
    pallas_call x1, Pallas kernels, local(): pl.pallas_call(functools.partial(finish, float((E * GX * GY) ** (-0.5))),...  2.86 us

profile of v7, /device:TPU:1, one launch (start us, length us, event | category | flops | bytes accessed | tf_op | source)
XLA Modules:
  0.0 56.8 jit_solution(7172374448355692526)
XLA Ops:
  0.6 53.1 %shard_map.137 = (bf16[32,256]{1,0:T(8,128)(2,1)}, bf16[2048,256]{1,0:T(8,128)(2,1)}, bf16[2,784,256]{2,1,0:T(8,128)(2,1)}) custom-call(bf16[2048,256]{1,0:T(8,128)(2,1)} %nodes_h.1, s32[1,128]{1,0:T(1,128)} %bitcast.6, s32[32,128]{1,0:T(8,128)} %src_h.1, s32[32,128]{1,0:T(8,128)} %tgt_h.1, s32[32,128]{1,0:T(8,128)} %mask_h.1, s32[16,128]{1,0:T(8,128)} %bitcast.4, ...), custom_call_target="tpu_custom_call" | custom-call | tf_op jit(solution)/shard_map/pallas_call | solution.py:831
  53.8 2.9 %shard_map.138 = (bf16[32,256]{1,0:T(8,128)(2,1)}, bf16[2048,256]{1,0:T(8,128)(2,1)}, f32[512,512]{1,0:T(8,128)}, f32[1,512]{1,0:T(1,128)}, f32[512,256]{1,0:T(8,128)}) custom-call(bf16[32,256]{1,0:T(8,128)(2,1)} %get-tuple-element.13.pooled, bf16[2048,256]{1,0:T(8,128)(2,1)} %get-tuple-element.14.gnodes, bf16[2,784,256]{2,1,0:T(8,128)(2,1)} %get-tuple-element.15.gw), custom_call_target="tpu_custom_call" | custom-call | tf_op jit(solution)/shard_map/pallas_call | solution.py:841
